TPU v7x, 128 devices: a whole 4x4x4 slice. The times are simulated.
128 devices in a mesh: dp: 32 (over y_hi, x, z), tensor: 4 (over y_lo, core).
Axes of the slice: x: 4, y: 4 (y_hi: 2, y_lo: 2; y = y_hi * 2 + y_lo), z: 4, core: 2. Of those that a mesh axis runs over, the one named last changes fastest.
Arguments:
- hidden_in: bfloat16 [16384, 2048], P(('dp', 'tensor')), may hold values from -6 to 6
- seq_lengths: int32 [32, 4], P('dp'), may hold values from 1 to 384, 512 in all within a row
- norm_gain: float32 [2048], P(('dp', 'tensor')), may hold values from 0.5 to 1.5
- norm_offset: float32 [2048], P(('dp', 'tensor')), may hold values from -3 to 3
- attn_weight: bfloat16 [3, 2048, 2048], P(None, 'dp', 'tensor'), may hold values from -0.125 to 0.125
- attn_bias: bfloat16 [3, 2048], P(None, ('tensor', 'dp')), may hold values from -3 to 3
- dense_weight: bfloat16 [2048, 2048], P('tensor', 'dp'), may hold values from -0.5 to 0.5
- dense_bias: bfloat16 [2048], P(('tensor', 'dp')), may hold values from -3 to 3
- expand_weight: bfloat16 [2048, 8192], P('dp', 'tensor'), may hold values from -0.125 to 0.125
- expand_bias: bfloat16 [8192], P(('tensor', 'dp')), may hold values from -3 to 3
- reduce_weight: bfloat16 [8192, 2048], P('tensor', 'dp'), may hold values from -0.0625 to 0.0625
- reduce_bias: bfloat16 [2048], P(('tensor', 'dp')), may hold values from -3 to 3
- out_grad: bfloat16 [16384, 2048], P(('dp', 'tensor')), may hold values from -6 to 6
Outputs:
- block_out: bfloat16 [16384, 2048], P(('dp', 'tensor'))
- input_grad: bfloat16 [16384, 2048], P(('dp', 'tensor'))
- norm_gain_grad: float32 [2048], P(('dp', 'tensor'))
- norm_offset_grad: float32 [2048], P(('dp', 'tensor'))
- attn_weight_grad: float32 [3, 2048, 2048], P(None, 'dp', 'tensor')
- attn_bias_grad: float32 [3, 2048], P(None, ('tensor', 'dp'))
- dense_weight_grad: float32 [2048, 2048], P('tensor', 'dp')
- dense_bias_grad: float32 [2048], P(('tensor', 'dp'))
- expand_weight_grad: float32 [2048, 8192], P('dp', 'tensor')
- expand_bias_grad: float32 [8192], P(('tensor', 'dp'))
- reduce_weight_grad: float32 [8192, 2048], P('tensor', 'dp')
- reduce_bias_grad: float32 [2048], P(('tensor', 'dp'))
Inputs may be any that keep to these rules, and one draw needn't show every extreme that they name: Each row of seq_lengths holds 4 lengths that sum to 512, the largest exactly 384.
All inputs are finite; a program needn't handle non-finite values.
Results may differ from a plain program's by a relative error of at most 0.013.
Values may be sent and summed in bfloat16 or wider, within the bound.
No kernel may reach another device: no remote copies, remote signals or barrier semaphores. Data moves between devices by JAX's collectives and lax.ppermute only.
A program may use at most 192 MiB of HBM per device.

v0:
```python
import numpy as np
import jax
import jax.numpy as jnp
from jax import lax
from jax.experimental import pallas as pl
from jax.experimental.pallas import tpu as pltpu
from jax.sharding import Mesh, PartitionSpec as P

HEAD_DIM = 64
ROT = 32
RING = 4
AXES = ("yhi", "x", "z", "ylo", "core")
COLUMN = ("yhi", "ylo", "core")
BF = jnp.bfloat16
F32 = jnp.float32
MIB = 1 << 20
BIG = 58
SMALL = 16


def ring_pairs(first_ring, step):
    pairs = []
    for x in range(RING):
        for z in range(RING):
            for core in range(2):
                along_x = (core == 0) == first_ring
                to_x = (x + step) % RING if along_x else x
                to_z = z if along_x else (z + step) % RING
                pairs.append(((x * RING + z) * 2 + core, (to_x * RING + to_z) * 2 + core))
    return pairs


def move(value, first_ring, step):
    return lax.ppermute(value, ("x", "z", "core"), ring_pairs(first_ring, step))


def axis_swaps(odd):
    return [(n, (n + (1 if n % 2 == odd else -1)) % RING) for n in range(RING)]


def move_y(value, step):
    pairs = [(y, (y + step) % RING) for y in range(RING)]
    return lax.ppermute(value, ("yhi", "ylo"), pairs)


def swap(value, axis):
    return lax.ppermute(value, axis, [(0, 1), (1, 0)])


def ring_send(blocks, first_ring, way):
    _, minus, plus, far = blocks
    direct = move(minus, first_ring, -1) if way > 0 else move(plus, first_ring, 1)
    return move(far, first_ring, way), direct


def ring_terms(blocks):
    here, minus, plus, far = blocks
    return here, move(minus, True, -1), move(plus, True, 1), move(far, True, 2)


ANY = pl.BlockSpec(memory_space=pl.ANY)
SMEM = pl.BlockSpec(memory_space=pltpu.SMEM)


def whole(shape):
    return pl.BlockSpec(shape, lambda *at: (0,) * len(shape))


def row_block(rows, cols):
    return pl.BlockSpec((rows, cols), lambda i: (i, 0))


def shaped(shape, dtype):
    return jax.ShapeDtypeStruct(shape, dtype)


def kernel_call(kernel, operands, waits, *, in_specs, **options):
    count, more = len(operands), len(waits)

    def run(*refs):
        kernel(*refs[:count], *refs[count + more :])

    in_specs = list(in_specs) + [ANY] * more
    scalars = count - len(in_specs) + more
    if scalars:
        parts = {key: options.pop(key) for key in ("grid", "out_specs", "scratch_shapes")}
        options["grid_spec"] = pltpu.PrefetchScalarGridSpec(
            num_scalar_prefetch=scalars, in_specs=in_specs, **parts
        )
    else:
        options["in_specs"] = in_specs
    return pl.pallas_call(run, **options)(*operands, *waits)


def parts_kernel(*refs):
    count = len(refs) // 2
    for ref, out in zip(refs[:count], refs[count:]):
        out[...] = ref[...]


def take_parts(*chosen):
    specs = [pl.BlockSpec(shape, lambda i, at=at: at) for _, shape, at in chosen]
    return kernel_call(
        parts_kernel,
        tuple(array for array, _, _ in chosen),
        (),
        grid=(1,),
        in_specs=specs,
        out_specs=tuple(whole(shape) for _, shape, _ in chosen),
        out_shape=tuple(shaped(shape, array.dtype) for array, shape, _ in chosen),
        compiler_params=params(SMALL),
        cost_estimate=cost(0, 4 * sum(int(np.prod(shape)) for _, shape, _ in chosen)),
        name="take_parts",
    )


def add_pairs_kernel(*refs):
    count = (len(refs) - 2) // 3
    for n in range(count):
        a, b, out = refs[2 * n], refs[2 * n + 1], refs[2 * count + 1 + n]
        out[...] = (a[...].astype(F32) + b[...].astype(F32)).astype(BF)


def add_pairs(pairs, carried, waits=()):
    shapes = [a.shape for a, _ in pairs]
    flat = [term.reshape(-1, term.shape[-1]) for pair in pairs for term in pair]
    halves = [row_block(term.shape[0] // 2, term.shape[1]) for term in flat]
    *sums, carried = kernel_call(
        add_pairs_kernel,
        (*flat, carried),
        waits,
        grid=(2,),
        in_specs=halves + [ANY],
        out_specs=tuple(halves[::2]) + (ANY,),
        out_shape=tuple(shaped(term.shape, BF) for term in flat[::2])
        + (shaped(carried.shape, carried.dtype),),
        input_output_aliases={len(flat): len(pairs)},
        compiler_params=params(BIG),
        cost_estimate=cost(0, 3 * sum(term.size for term in flat)),
        name="add_pairs",
    )
    return [total.reshape(shape) for total, shape in zip(sums, shapes)] + [carried]


def add_lines_kernel(*refs):
    outs = refs[-RING:]
    sources, at = refs[:-RING], 0
    for n in range(0, len(sources), 3):
        total = sum(ref[...].astype(F32) for ref in sources[n : n + 3])
        for i, out in enumerate(outs):
            out[:, at : at + total.shape[-1]] = total[i].astype(BF)
        at += total.shape[-1]


def add_lines(lines, waits=()):
    operands = [term for terms in lines for term in terms]
    rows = operands[0].shape[1]
    cols = sum(terms[0].shape[2] for terms in lines)
    at_once = rows // 2
    specs = [
        pl.BlockSpec((RING, at_once, term.shape[2]), lambda i: (0, i, 0)) for term in operands
    ]
    return kernel_call(
        add_lines_kernel,
        tuple(operands),
        waits,
        grid=(2,),
        in_specs=specs,
        out_specs=(row_block(at_once, cols),) * RING,
        out_shape=(shaped((rows, cols), BF),) * RING,
        compiler_params=params(SMALL),
        cost_estimate=cost(0, 8 * RING * rows * cols),
        name="add_lines",
    )


def finish_kernel(count, at_yhi, *refs):
    outs = refs[count * (len(refs) // (count + 1)) :]
    for n, out in enumerate(outs):
        total = sum(ref[...].astype(F32) for ref in refs[n * count : (n + 1) * count])
        out[...] = total.astype(out.dtype)


def finish_sums(at_yhi, terms, cols, waits=()):
    rows, more = terms[0].shape[0], terms[0].shape[1] - cols
    half = rows // 2
    keep = pl.BlockSpec((half, cols), lambda i, at: (at[0], 0))
    send = pl.BlockSpec((half, cols), lambda i, at: (1 - at[0], 0))
    out = pl.BlockSpec((half, cols), lambda i, at: (0, 0))
    count = len(terms)
    specs, outs = [keep] * count + [send] * count, [out] * 2
    shapes = [shaped((half, cols), F32), shaped((half, cols), BF)]
    if more:
        specs += [pl.BlockSpec((rows, more), lambda i, at: (0, cols // more))] * count
        outs.append(pl.BlockSpec((rows, more), lambda i, at: (0, 0)))
        shapes.append(shaped((rows, more), F32))

    def kernel(*refs):
        finish_kernel(count, *refs)

    return kernel_call(
        kernel,
        (at_yhi, *(tuple(terms) * (len(specs) // count))),
        waits,
        grid=(1,),
        in_specs=specs,
        out_specs=tuple(outs),
        out_shape=tuple(shapes),
        scratch_shapes=(),
        compiler_params=params(SMALL),
        cost_estimate=cost(0, 8 * rows * cols),
        name="finish_sums",
    )


def join_kernel(layout, at_yhi, keep, got, *outs):
    part = jnp.where(pl.program_id(0) == 0, keep[...], got[...].astype(F32))
    for (count, first, width), out in zip(layout, outs):
        for n in range(count):
            block = part[:, first + n * width : first + (n + 1) * width]
            if len(out.shape) == 3:
                out[n] = block
            else:
                out[...] = block


def join_halves(at_yhi, keep, got, layout, waits=()):
    rows, cols = keep.shape

    def kernel(*refs):
        join_kernel(layout, *refs)

    def side(i, at):
        return at[0] + i * (1 - 2 * at[0])

    specs, shapes = [], []
    for count, _, width in layout:
        lead = (count,) if count > 1 else ()
        zeros = (0,) * (len(lead) + 1)
        specs.append(
            pl.BlockSpec(lead + (rows, width), lambda i, at, zeros=zeros: (*zeros, side(i, at)))
        )
        shapes.append(shaped(lead + (rows, 2 * width), F32))
    here = pl.BlockSpec((rows, cols), lambda i, at: (0, 0))
    return kernel_call(
        kernel,
        (at_yhi, keep, got),
        waits,
        grid=(2,),
        in_specs=[here, here],
        out_specs=tuple(specs),
        out_shape=tuple(shapes),
        scratch_shapes=(),
        compiler_params=params(BIG),
        cost_estimate=cost(0, 12 * rows * cols),
        name="join_halves",
    )


def params(megabytes):
    return pltpu.CompilerParams(vmem_limit_bytes=megabytes * MIB)


def cost(flops, moved, special=0):
    return pl.CostEstimate(flops=flops, bytes_accessed=moved, transcendentals=special)


def dot_nn(a, b):
    return jnp.dot(a, b, preferred_element_type=F32)


def dot_nt(a, b):
    return lax.dot_general(a, b, (((1,), (1,)), ((), ())), preferred_element_type=F32)


def dot_tn(a, b):
    return lax.dot_general(a, b, (((0,), (0,)), ((), ())), preferred_element_type=F32)


def split_kernel(at_yhi, *refs):
    ins, outs = refs[:8], refs[8:]
    for n, out in enumerate(outs):
        attn, *others = ins[4 * n : 4 * n + 4]
        at = 0
        for part in [attn[j] for j in range(3)] + [ref[...] for ref in others]:
            out[:, at : at + part.shape[1]] = part
            at += part.shape[1]


def split_columns(at_yhi, attn, dense, expand, reduce):
    rows, cols = expand.shape[0], expand.shape[1] // 2
    ins = []
    for n in range(2):

        def side(at, n=n):
            return at[0] if n == 0 else 1 - at[0]

        ins.append(pl.BlockSpec((3, rows, cols // 4), lambda i, at, side=side: (0, 0, side(at))))
        for width in (cols // 4, cols, cols):
            ins.append(pl.BlockSpec((rows, width), lambda i, at, side=side: (0, side(at))))
    return pl.pallas_call(
        split_kernel,
        grid_spec=pltpu.PrefetchScalarGridSpec(
            num_scalar_prefetch=1,
            grid=(1,),
            in_specs=ins,
            out_specs=(whole((rows, 3 * cols)),) * 2,
        ),
        out_shape=(shaped((rows, 3 * cols), BF),) * 2,
        compiler_params=params(BIG),
        cost_estimate=cost(0, 6 * rows * cols * 4),
        name="split_columns",
    )(at_yhi, *[attn, dense, expand, reduce] * 2)


def paired(rows):
    lanes = 2 * HEAD_DIM
    low = lax.broadcasted_iota(jnp.int32, (rows.shape[0], lanes), 1) < HEAD_DIM
    half = rows.shape[1] // 2
    for k in range(half // lanes):
        a = rows[:, k * lanes : (k + 1) * lanes]
        b = rows[:, half + k * lanes : half + (k + 1) * lanes]
        yield 2 * k * lanes, jnp.where(low, a, pltpu.roll(b, HEAD_DIM, 1))
        yield (2 * k + 1) * lanes, jnp.where(low, pltpu.roll(a, HEAD_DIM, 1), b)


def unpaired(rows):
    lanes = 2 * HEAD_DIM
    low = lax.broadcasted_iota(jnp.int32, (rows.shape[0], lanes), 1) < HEAD_DIM
    half = rows.shape[1] // 2
    for k in range(half // lanes):
        a = rows[:, 2 * k * lanes : (2 * k + 1) * lanes]
        b = rows[:, (2 * k + 1) * lanes : (2 * k + 2) * lanes]
        yield k * lanes, jnp.where(low, a, pltpu.roll(b, HEAD_DIM, 1))
        yield half + k * lanes, jnp.where(low, pltpu.roll(a, HEAD_DIM, 1), b)


def pair_kernel(hidden, grad, out):
    for n, ref in enumerate((hidden, grad)):
        for at, block in paired(ref[...].astype(F32)):
            out[n, :, at : at + block.shape[1]] = block.astype(BF)


def pair_columns(hidden, grad, *waits):
    rows, width = hidden.shape
    at_once = rows // 2
    return kernel_call(
        pair_kernel,
        (hidden, grad),
        waits,
        grid=(2,),
        in_specs=[row_block(at_once, width)] * 2,
        out_specs=pl.BlockSpec((2, at_once, width), lambda i: (0, i, 0)),
        out_shape=shaped((2, rows, width), BF),
        compiler_params=params(SMALL),
        cost_estimate=cost(0, 8 * rows * width),
        name="pair_columns",
    )


def output_kernel(hidden, branch, out):
    total = hidden[0].astype(F32) + branch[...].astype(F32)
    for at, block in unpaired(total):
        out[:, at : at + block.shape[1]] = block.astype(BF)


def own_block(which, rows, width):
    return pl.BlockSpec((1, rows, width), lambda i: (which, i, 0))


def output_layer(own, branch, *waits):
    _, rows, width = own.shape
    at_once = rows // 2
    return kernel_call(
        output_kernel,
        (own, branch),
        waits,
        grid=(2,),
        in_specs=[own_block(0, at_once, width), row_block(at_once, width)],
        out_specs=row_block(at_once, width),
        out_shape=shaped((rows, width), BF),
        compiler_params=params(SMALL),
        cost_estimate=cost(0, 6 * rows * width),
        name="output",
    )


def input_grad_kernel(hidden, grad, normed_grad, small, out):
    rows = hidden[0].astype(F32)
    center = rows - jnp.mean(rows, -1, keepdims=True)
    spread = lax.rsqrt(jnp.mean(center * center, -1, keepdims=True) + 1e-05)
    x_hat = center * spread
    gain, _ = norm_rows(small)
    scaled = normed_grad[...].astype(F32) * gain
    total = grad[0].astype(F32) + spread * (
        scaled
        - jnp.mean(scaled, -1, keepdims=True)
        - x_hat * jnp.mean(scaled * x_hat, -1, keepdims=True)
    )
    for at, block in unpaired(total):
        out[:, at : at + block.shape[1]] = block.astype(BF)


def input_grad_layer(own, normed_grad, small, *waits):
    _, rows, width = own.shape
    at_once = rows // 2
    return kernel_call(
        input_grad_kernel,
        (own, own, normed_grad, small),
        waits,
        grid=(2,),
        in_specs=[own_block(n, at_once, width) for n in range(2)]
        + [row_block(at_once, width), whole(small.shape)],
        out_specs=row_block(at_once, width),
        out_shape=shaped((rows, width), BF),
        compiler_params=params(SMALL),
        cost_estimate=cost(0, 8 * rows * width),
        name="input_grad",
    )


def put_in_turn(rows, turned, out):
    lanes = 2 * HEAD_DIM
    for n in range(rows.shape[1] // lanes):
        at = pl.multiple_of(turned[n] * lanes, lanes)
        out[:, pl.ds(at, lanes)] = rows[:, n * lanes : (n + 1) * lanes].astype(out.dtype)


def fold(small):
    return small.reshape(16, -1, 128).transpose(1, 0, 2).reshape(-1, 128)


def unfold(small):
    return small.reshape(-1, 16, 128).transpose(1, 0, 2).reshape(16, -1)


def norm_rows(small):
    def row(at):
        return small[at : at + 1] + small[at + 1 : at + 2] + small[at + 2 : at + 3]

    gain = jnp.concatenate([row(0), row(6)], 1)
    offset = jnp.concatenate([row(3), row(9)], 1)
    return gain, offset


def load_rows(chips, sources, held, sems, step):
    copies = []
    for n, ref in enumerate(sources):
        core = chips[RING] if n % 2 == 0 else 1 - chips[RING]
        copies.append(pltpu.make_async_copy(ref, held.at[n // 2, core], sems.at[n]))

    @pl.when(step == 0)
    def _():
        for copy in copies:
            copy.start()

    for n in range(RING):

        @pl.when(step == n)
        def _(n=n):
            copies[2 * n].wait()
            copies[2 * n + 1].wait()

    rows = held[step]
    return rows.reshape(-1, rows.shape[-1])


def chip_block(rows, cols):
    return pl.BlockSpec((rows, cols), lambda i, chips: (chips[i], 0))


def prefetched(specs):
    return [
        spec
        if spec.index_map is None
        else pl.BlockSpec(spec.block_shape, lambda i, chips, at=spec.index_map: at(i))
        for spec in specs
    ]


def rows_kernel(chips, turned, small, *refs):
    sources, rest = refs[: 2 * RING], refs[2 * RING :]
    normed, normed_turned, x_hat, grad, grad_turned, grad_sum, held, grad_held, sems, grad_sems = rest
    step = pl.program_id(0)

    @pl.when(step == 0)
    def _():
        grad_sum[...] = jnp.zeros_like(grad_sum)

    rows = load_rows(chips, [hidden_of(ref) for ref in sources], held, sems, step).astype(F32)
    gain, offset = norm_rows(small)
    center = rows - jnp.mean(rows, -1, keepdims=True)
    scaled = center * lax.rsqrt(jnp.mean(center * center, -1, keepdims=True) + 1e-05)
    x_hat[...] = scaled.astype(BF)
    normed[...] = (scaled * gain + offset).astype(BF)
    put_in_turn(normed, turned, normed_turned)
    rows = load_rows(chips, [grad_of(ref) for ref in sources], grad_held, grad_sems, step)
    grad[...] = rows
    put_in_turn(grad, turned, grad_turned)
    grad_sum[...] += jnp.sum(rows.astype(F32), 0, keepdims=True)


def hidden_of(ref):
    return ref.at[0] if len(ref.shape) == 3 else ref


def grad_of(ref):
    return ref.at[1] if len(ref.shape) == 3 else ref


def rows_layer(chips, turned, small, sources, *waits):
    local_rows, width = sources[0].shape[-2:]
    rows = 2 * RING * local_rows
    at_once = 2 * local_rows
    return kernel_call(
        rows_kernel,
        (chips, turned, small, *sources),
        waits,
        grid=(RING,),
        in_specs=[SMEM] + prefetched([whole(small.shape)]) + [ANY] * len(sources),
        out_specs=(chip_block(at_once, width),) * 5 + tuple(prefetched([whole((1, width))])),
        out_shape=(shaped((rows, width), BF),) * 5 + (shaped((1, width), F32),),
        scratch_shapes=[pltpu.VMEM((RING, 2, local_rows, width), BF)] * 2
        + [pltpu.SemaphoreType.DMA((2 * RING,))] * 2,
        compiler_params=params(BIG),
        cost_estimate=cost(0, 14 * rows * width),
        name="rows",
    )


def expand_kernel(weight, qkv_w, normed, small, activated, slope, projected):
    projected[...] = dot_nn(normed[...], qkv_w[...]) + small[12:13, : projected.shape[1]]
    u = dot_nn(normed[...], weight[...]) + small[14:15]
    factor = (2.0 / np.pi) ** 0.5
    square = u * u
    bent = jnp.tanh(factor * u * (1.0 + 0.044715 * square))
    half = 0.5 + 0.5 * bent
    activated[...] = (u * half).astype(BF)
    rise = factor * (1.0 + 3.0 * 0.044715 * square)
    slope[...] = (half + 0.5 * u * (1.0 - bent * bent) * rise).astype(BF)


def expand_layer(weights, normed, small, *waits):
    rows, width = normed.shape
    cols = weights.shape[1] // 3
    three = cols // 4 * 3
    at_once = 256
    return kernel_call(
        expand_kernel,
        (weights, weights, normed, small),
        waits,
        grid=(rows // at_once,),
        in_specs=[
            pl.BlockSpec((width, cols), lambda i: (0, 1)),
            pl.BlockSpec((width, three), lambda i: (0, 0)),
            row_block(at_once, width),
            whole(small.shape),
        ],
        out_specs=(row_block(at_once, cols),) * 2 + (row_block(at_once, three),),
        out_shape=(shaped((rows, cols), BF),) * 2 + (shaped((rows, three), F32),),
        compiler_params=params(BIG),
        cost_estimate=cost(2 * rows * width * (cols + three), 4 * rows * width, rows * cols),
        name="expand",
    )


def feed_back_kernel(weights, grad, slope, normed, activated, grad_turned, *refs):
    eg_out, bias_grad, attended_grad, *outs = refs[: 3 + 2 * RING]
    weight_v, dense_v, grad_v, slope_v, normed_v, activated_v, turned_v, eg_v, hold, *rest = refs[
        3 + 2 * RING :
    ]
    sems, out_sems = rest
    step = pl.program_id(0)
    tile = grad.shape[0] // RING
    quarter = grad.shape[1] // RING

    def loads():
        cols = weight_v.shape[1]
        made = [(weights.at[:, pl.ds(2 * cols, cols)], weight_v)]
        for n in range(RING):
            made.append((grad.at[pl.ds(n * tile, tile)], grad_v.at[pl.ds(n * tile, tile)]))
        made += [
            (slope, slope_v), (normed, normed_v), (activated, activated_v), (grad_turned, turned_v),
            (weights.at[:, pl.ds(cols - dense_v.shape[1], dense_v.shape[1])], dense_v),
        ]
        return [pltpu.make_async_copy(a, b, sems.at[n]) for n, (a, b) in enumerate(made)]

    def stores():
        made = [pltpu.make_async_copy(hold.at[n], out, out_sems.at[n]) for n, out in enumerate(outs)]
        return made + [pltpu.make_async_copy(eg_v, eg_out, out_sems.at[2 * RING])]

    @pl.when(step == 0)
    def _():
        copies = loads()
        for n in (0, 1, 5, 9, 2, 3, 4, 6, 7, 8):
            copies[n].start()
        copies[0].wait()
        copies[5].wait()
        copies[9].wait()
        bias_grad[...] = jnp.zeros_like(bias_grad)

    for n in range(RING):

        @pl.when(step == n)
        def _(n=n):
            loads()[1 + n].wait()

    @pl.when(step < RING)
    def _():
        at = pl.ds(pl.multiple_of(step * tile, tile), tile)
        low = dot_nn(grad_v[at, :], weight_v[...]) * slope_v[at, :].astype(F32)
        low = low.astype(BF)
        eg_v[at, :] = low
        attended_grad[at, :] = dot_nn(grad_v[at, :], dense_v[...]).astype(BF)
        bias_grad[...] += jnp.sum(low.astype(F32), 0, keepdims=True)

    @pl.when(step == RING)
    def _():
        stores()[2 * RING].start()
        loads()[6].wait()

    @pl.when(step == 2 * RING)
    def _():
        loads()[7].wait()
        loads()[8].wait()

    def columns(first):
        return pl.ds(pl.multiple_of((step - first) * quarter, quarter), quarter)

    @pl.when((step >= RING) & (step < 2 * RING))
    def _():
        hold[step - RING] = dot_tn(normed_v[:, columns(RING)], eg_v[...]).astype(BF)

    @pl.when(step >= 2 * RING)
    def _():
        hold[step - RING] = dot_tn(turned_v[:, columns(2 * RING)], activated_v[...]).astype(BF)

    for n in range(2 * RING):

        @pl.when(step == n + RING)
        def _(n=n):
            stores()[n].start()

    @pl.when(step == 3 * RING - 1)
    def _():
        for copy in stores():
            copy.wait()


def feed_back(weights, grad, slope, normed, activated, grad_turned, *waits):
    rows, width = grad.shape
    cols = weights.shape[1] // 3
    depth = width // RING
    outs = kernel_call(
        feed_back_kernel,
        (weights, grad, slope, normed, activated, grad_turned),
        waits,
        grid=(3 * RING,),
        in_specs=[ANY] * 6,
        out_specs=(ANY, whole((1, cols)), whole((rows, cols // 4))) + (ANY,) * (2 * RING),
        out_shape=(shaped((rows, cols), BF), shaped((1, cols), F32), shaped((rows, cols // 4), BF))
        + (shaped((depth, cols), BF),) * (2 * RING),
        scratch_shapes=[
            pltpu.VMEM((width, cols), BF),
            pltpu.VMEM((width, cols // 4), BF),
            pltpu.VMEM((rows, width), BF),
            pltpu.VMEM((rows, cols), BF),
            pltpu.VMEM((rows, width), BF),
            pltpu.VMEM((rows, cols), BF),
            pltpu.VMEM((rows, width), BF),
            pltpu.VMEM((rows, cols), BF),
            pltpu.VMEM((2 * RING, depth, cols), BF),
            pltpu.SemaphoreType.DMA((RING + 6,)),
            pltpu.SemaphoreType.DMA((2 * RING + 1,)),
        ],
        compiler_params=params(BIG),
        cost_estimate=cost(6 * rows * width * cols, 20 * rows * width),
        name="feed_back",
    )
    quarters = [quarter.reshape(RING, -1, cols) for quarter in outs[3:]]
    return *outs[:3], quarters[:RING], quarters[RING:]


def branch_kernel(rank, dense, reduce, activated, attended, small, branch, bias):
    heads = attended.shape[1]
    lanes = 2 * HEAD_DIM

    @pl.when(pl.program_id(0) == 0)
    def _():
        mine = small[12:13, 3 * heads :] + small[13:14, 3 * heads :]
        lane = lax.broadcasted_iota(jnp.int32, (1, lanes), 1)
        places = heads // HEAD_DIM
        side = (lane // HEAD_DIM) == rank[0] // (RING * RING // places)
        for n in range(RING * RING):
            part = mine[:, (n % places) * HEAD_DIM : (n % places + 1) * HEAD_DIM]
            part = jnp.concatenate([part, part], 1)
            here = rank[0] % (RING * RING // places) == n // places
            bias[:, n * lanes : (n + 1) * lanes] = jnp.where(side & here, part, 0.0)

    total = dot_nt(activated[...], reduce[...]) + dot_nt(attended[...], dense[...])
    branch[...] = (total + bias[...]).astype(BF)


def branch_layer(rank, activated, attended, weights, small, *waits):
    rows, cols = activated.shape
    heads = attended.shape[1]
    width = weights.shape[0]
    at_once = 256
    return kernel_call(
        branch_kernel,
        (rank, weights, weights, activated, attended, small),
        waits,
        grid=(rows // at_once,),
        in_specs=[SMEM]
        + [pl.BlockSpec((width, heads), lambda i: (0, 3))]
        + [pl.BlockSpec((width, cols), lambda i: (0, 2))]
        + [row_block(at_once, cols), row_block(at_once, heads), whole(small.shape)],
        out_specs=row_block(at_once, width),
        out_shape=shaped((rows, width), BF),
        scratch_shapes=[pltpu.VMEM((1, width), F32)],
        compiler_params=params(BIG),
        cost_estimate=cost(
            2 * rows * width * (cols + heads), 2 * (width + rows) * (cols + heads) + 2 * rows * width
        ),
        name="branch",
    )


def normed_grad_kernel(qkv_w, expand_w, proj_grad, expanded_grad, x_hat, part, sums):
    @pl.when(pl.program_id(0) == 0)
    def _():
        sums[...] = jnp.zeros_like(sums)

    total = dot_nt(proj_grad[...], qkv_w[...]) + dot_nt(expanded_grad[...], expand_w[...])
    part[...] = total.astype(BF)
    gain = jnp.sum(total * x_hat[...].astype(F32), 0, keepdims=True)
    offset = jnp.sum(total, 0, keepdims=True)
    sums[...] += jnp.concatenate([gain, offset], 0)


def normed_grad_layer(proj_grad, expanded_grad, weights, x_hat, *waits):
    rows, width = x_hat.shape
    cols, three = expanded_grad.shape[1], proj_grad.shape[1]
    depth = width // RING
    at_once = 256
    return kernel_call(
        normed_grad_kernel,
        (weights, weights, proj_grad, expanded_grad, x_hat),
        waits,
        grid=(rows // at_once,),
        in_specs=[pl.BlockSpec((width, three), lambda i: (0, 0))]
        + [pl.BlockSpec((width, cols), lambda i: (0, 1))]
        + [row_block(at_once, three), row_block(at_once, cols), row_block(at_once, width)],
        out_specs=(row_block(at_once, width), whole((2, width))),
        out_shape=(shaped((rows, width), BF), shaped((2, width), F32)),
        compiler_params=params(BIG),
        cost_estimate=cost(
            2 * rows * width * (cols + three), 2 * (width + rows) * (cols + three) + 4 * rows * width
        ),
        name="normed_grad",
    )


def weight_grad_kernel(count, *refs):
    lefts, rights = refs[:count], refs[count : 2 * count]
    *small, out0, out1, out2, out3, hold, sems = refs[2 * count :]
    outs = (out0, out1, out2, out3)
    step, last = pl.program_id(0), pl.num_programs(0) - 1
    cols = 0
    for a, b in zip(lefts, rights):
        hold[step, :, cols : cols + b.shape[1]] = dot_tn(a[...], b[...]).astype(BF)
        cols += b.shape[1]
    for ref in small:
        for n in range(RING):
            lanes = ref.shape[1]
            hold[step, n * lanes : (n + 1) * lanes, cols:] = ref[...]
    for n, out in enumerate(outs):

        @pl.when(step == n)
        def _(n=n, out=out):
            pltpu.make_async_copy(hold.at[n], out, sems.at[n]).start()

    @pl.when(step == last)
    def _():
        for n, out in enumerate(outs):
            pltpu.make_async_copy(hold.at[n], out, sems.at[n]).wait()


def weight_grad(pairs, small=None, waits=()):
    rows, width = pairs[0][0].shape
    more = [] if small is None else [small]
    cols = sum(right.shape[1] for _, right in pairs) + sum(extra.shape[1] for extra in more)
    at_once = width // RING

    def kernel(*refs):
        weight_grad_kernel(len(pairs), *refs)

    left = pl.BlockSpec((rows, at_once), lambda i: (0, i))
    quarters = kernel_call(
        kernel,
        (*[a for a, _ in pairs], *[b for _, b in pairs], *more),
        waits,
        grid=(RING,),
        in_specs=[left] * len(pairs)
        + [whole(right.shape) for _, right in pairs]
        + [whole(extra.shape) for extra in more],
        out_specs=(ANY,) * RING,
        out_shape=(shaped((at_once, cols), BF),) * RING,
        scratch_shapes=[
            pltpu.VMEM((RING, at_once, cols), BF),
            pltpu.SemaphoreType.DMA((RING,)),
        ],
        compiler_params=params(BIG),
        cost_estimate=cost(
            2 * rows * width * cols, 2 * (len(pairs) * rows * width + rows * cols + width * cols)
        ),
        name="weight_grad",
    )
    return [quarter.reshape(RING, -1, cols) for quarter in quarters]


def rolled(value, shift):
    return pltpu.roll(value, shift % value.shape[-1], value.ndim - 1)


def rotate(value, cos, sin_low, sin_high, sign):
    half = ROT // 2
    turned = rolled(value, -half) * sin_low + rolled(value, half) * sin_high
    return value * cos + sign * turned


def attention_kernel(
    projected, out_grad, cos, sin_low, sin_high, start, mixed, proj_grad, bias_grad
):
    rows, width = out_grad.shape
    heads = width // HEAD_DIM
    scale = HEAD_DIM**-0.5
    tables = [
        jnp.concatenate([ref[...]] * (width // ref.shape[1]), 1) for ref in (cos, sin_low, sin_high)
    ]
    query_rot = (rotate(projected[:, :width], *tables, 1.0).astype(BF) * scale).astype(BF)
    key_rot = rotate(projected[:, width : 2 * width], *tables, 1.0).astype(BF)
    value_rows = projected[:, 2 * width :].astype(BF)
    grad_rows = out_grad[...]
    half = rows // 4
    lane = lax.broadcasted_iota(jnp.int32, (half, width), 1)
    mine = [(lane >= h * HEAD_DIM) & (lane < (h + 1) * HEAD_DIM) for h in range(heads)]

    def stacked(block):
        return jnp.concatenate([jnp.where(m, block, jnp.zeros_like(block)) for m in mine], 0)

    def gathered(stack):
        total = None
        for h in range(heads):
            part = stack[h * half : (h + 1) * half]
            total = part if total is None else jnp.where(mine[h], part, total)
        return total

    key_sum, value_sum = {}, {}
    for first in range(0, rows, half):
        last = first + half
        here = slice(first, last)
        row_id = lax.broadcasted_iota(jnp.int32, (half, last), 0) + first
        col_id = lax.broadcasted_iota(jnp.int32, (half, last), 1)
        allowed = ((col_id <= row_id) & (col_id >= start[here, 0:1]))[None]
        queries, grads = stacked(query_rot[here]), stacked(grad_rows[here])
        scores = dot_nt(queries, key_rot[:last]).reshape(heads, half, last)
        scores = jnp.where(allowed, scores, -1000000000.0)
        top = jnp.max(scores, -1, keepdims=True)
        expd = jnp.exp(scores - top)
        probs = expd * (1.0 / jnp.sum(expd, -1, keepdims=True))
        prob_low = probs.astype(BF).reshape(heads * half, last)
        prob_grad = dot_nt(grads, value_rows[:last]).reshape(heads, half, last)
        row_dot = jnp.sum(probs * prob_grad, -1, keepdims=True)
        score_grad = (probs * (prob_grad - row_dot)).astype(BF).reshape(heads * half, last)
        mixed[here, :] = gathered(dot_nn(prob_low, value_rows[:last])).astype(BF)
        query_part = gathered(dot_nn(score_grad, key_rot[:last])) * scale
        query_part = rotate(query_part, *[table[here] for table in tables], -1.0).astype(BF)
        proj_grad[here, :width] = query_part
        query_bias = jnp.sum(query_part.astype(F32), 0, keepdims=True)
        bias_grad[0, :, :width] = query_bias if first == 0 else bias_grad[0, :, :width] + query_bias
        key_part, value_part = dot_tn(score_grad, queries), dot_tn(prob_low, grads)
        for n in range(0, last, half):
            for sums, part in ((key_sum, key_part), (value_sum, value_part)):
                block = part[n : n + half]
                sums[n] = sums[n] + block if n in sums else block
    for j, sums in ((1, key_sum), (2, value_sum)):
        total = jnp.concatenate([sums[n] for n in range(0, rows, half)], 0)
        if j == 1:
            total = rotate(total, *tables, -1.0)
        low = total.astype(BF)
        proj_grad[:, j * width : (j + 1) * width] = low
        bias_grad[0, :, j * width : (j + 1) * width] = jnp.sum(low.astype(F32), 0, keepdims=True)


def attention(projected, out_grad, cos, sin_low, sin_high, start, pack_rows, *waits):
    rows, width = out_grad.shape
    lanes = cos.shape[1]
    packs = rows // pack_rows
    return kernel_call(
        attention_kernel,
        (projected, out_grad, cos, sin_low, sin_high, start),
        waits,
        grid=(packs,),
        in_specs=[row_block(pack_rows, 3 * width), row_block(pack_rows, width)]
        + [row_block(pack_rows, lanes)] * 4,
        out_specs=(
            row_block(pack_rows, width),
            row_block(pack_rows, 3 * width),
            pl.BlockSpec((1, 1, 3 * width), lambda p: (p, 0, 0)),
        ),
        out_shape=(
            shaped((rows, width), BF),
            shaped((rows, 3 * width), BF),
            shaped((packs, 1, 3 * width), F32),
        ),
        compiler_params=params(BIG),
        cost_estimate=cost(
            14 * rows * pack_rows * width, rows * width * 32, rows * pack_rows * width // HEAD_DIM
        ),
        name="attention",
    )


def pick(first, a, b):
    return jnp.where(first, a, b), jnp.where(first, b, a)


def three_parts(value):
    high = lax.reduce_precision(value, 8, 7)
    rest = value - high
    mid = lax.reduce_precision(rest, 8, 7)
    return [high, mid, rest - mid]


def body(
    hidden_in,
    seq_lengths,
    norm_gain,
    norm_offset,
    attn_weight,
    attn_bias,
    dense_weight,
    dense_bias,
    expand_weight,
    expand_bias,
    reduce_weight,
    reduce_bias,
    out_grad,
):
    at_yhi, at_x, at_z, at_ylo, at_core = (lax.axis_index(a) for a in AXES)
    first_yhi, first_ylo, first_core = at_yhi == 0, at_ylo == 0, at_core == 0
    local_rows, width = hidden_in.shape
    pack_rows = local_rows * RING
    at_tensor = at_ylo * 2 + at_core
    column_rank = at_tensor * 2 + at_yhi
    plane = RING * RING
    at_plane = at_x * RING + at_z

    place = np.arange(plane, dtype=np.int32)
    x, z = (place // RING - at_x) % RING, (place % RING - at_z) % RING
    inner, outer = jnp.where(first_core, x, z), jnp.where(first_core, z, x)
    order = np.array([0, 2, 3, 1], np.int32)

    def position(step):
        return sum(jnp.where(step == n, order[n], 0) for n in range(1, RING))

    turned = (position(outer) * RING + position(inner)).astype(jnp.int32)

    lanes = 2 * HEAD_DIM
    block_rows, cols = expand_weight.shape[0], expand_weight.shape[1] // 2
    heads = cols // 4

    unit = norm_gain.shape[0]
    norms = jnp.stack(three_parts(norm_gain) + three_parts(norm_offset))
    lengths = seq_lengths[0]
    count = lengths.shape[0]
    small = lax.dynamic_update_slice(
        jnp.zeros((16, cols), F32),
        norms,
        (at_plane // 8 * 6, at_plane % 8 * 8 * unit + at_yhi * 4 * unit + at_tensor * unit),
    )
    two = jnp.concatenate([lengths // 16, lengths % 16]).astype(F32)
    small = lax.dynamic_update_slice(small, two[None], (15, at_yhi * 2 * count)).astype(BF)

    own, other = split_columns(
        at_yhi.reshape(1).astype(jnp.int32),
        attn_weight, dense_weight.T, expand_weight, reduce_weight.T,
    )
    got = swap(other, "yhi")
    block = jnp.concatenate(pick(first_yhi, own, got), 0)
    weights = lax.all_gather(block, ("x", "z"), axis=0, tiled=True)

    small = small + swap(small, "yhi")
    two = small[15, : 4 * count].astype(F32).reshape(2, 2, count)
    length_rows = (two[:, 0] * 16.0 + two[:, 1]).astype(jnp.int32)
    biases = jnp.stack([dense_bias, reduce_bias])
    biases = jnp.concatenate([jnp.stack([attn_bias, 0 * attn_bias]), biases[:, None]], 1)
    bias_rows = lax.dynamic_update_slice(
        jnp.zeros((2, 4, heads), BF), biases, (0, 0, at_plane * unit)
    ).reshape(2, cols)
    expand_row = lax.dynamic_update_slice(
        jnp.zeros((2, cols), BF), expand_bias[None], (0, at_plane * expand_bias.shape[0])
    )
    small = jnp.concatenate([small[:12], bias_rows, expand_row], 0)

    for axis in ("x", "z"):
        for odd in range(2):
            small = small + lax.ppermute(small, axis, axis_swaps(odd))
    parts = jnp.where((np.arange(16) < 12)[:, None], small, jnp.zeros_like(small))
    others = swap(parts, "ylo")
    small = (small + others + swap(parts + others, "core")).astype(F32)

    own_rows = pair_columns(hidden_in, out_grad, got)
    below, above = move_y(own_rows, 1), move_y(own_rows, -1)
    one = (1,) + own_rows.shape[1:]
    far_hidden, far_grad = take_parts((below, one, (0, 0, 0)), (above, one, (1, 0, 0)))
    far_hidden, far_grad = move_y(far_hidden, 1), move_y(far_grad, -1)
    far_rows = jnp.concatenate([far_hidden, far_grad], 0)
    sources = [
        ref for rows in (own_rows, below, above, far_rows) for ref in (rows, swap(rows, "core"))
    ]
    at_y = at_yhi * 2 + at_ylo
    chips = jnp.stack([at_y, (at_y + 3) % RING, (at_y + 1) % RING, (at_y + 2) % RING, at_core])
    chips = chips.astype(jnp.int32)

    ends = jnp.cumsum(length_rows, 1)
    row_ids = jnp.arange(pack_rows, dtype=jnp.int32)
    begun = row_ids[None, :, None] >= ends[:, None, :]
    start = jnp.max(jnp.where(begun, ends[:, None, :], 0), 2).reshape(-1, 1)
    position = (jnp.tile(row_ids, 2)[:, None] - start).astype(F32)
    lane = np.arange(lanes) % HEAD_DIM
    half = ROT // 2
    inverse = np.float32(10000.0) ** (np.float32(-2.0) * (lane % half).astype(np.float32) / ROT)
    angles = position * inverse.astype(np.float32)[None, :]
    cos = jnp.where((lane < ROT)[None, :], jnp.cos(angles), 1.0)
    sine = jnp.sin(angles)
    sin_low = jnp.where((lane < half)[None, :], -sine, 0.0)
    sin_high = jnp.where(((lane >= half) & (lane < ROT))[None, :], sine, 0.0)
    start = jnp.broadcast_to(start, (start.shape[0], lanes))

    normed, normed_turned, x_hat, grad_all, grad_turned, grad_sum = rows_layer(
        chips, turned, small, sources, cos, sin_low, sin_high, start
    )
    activated, slope, projected = expand_layer(weights, normed, small)
    expanded_grad, expand_bias_grad, attended_grad, expand_1, reduce_1 = feed_back(
        weights, grad_all, slope, normed_turned, activated, grad_turned
    )
    expand_sent = ring_send(expand_1, False, 1)
    reduce_sent = ring_send(reduce_1, False, -1)
    attended, proj_grad, attn_bias_grad = attention(
        projected, attended_grad, cos, sin_low, sin_high, start, pack_rows
    )
    normed_part, norm_sums = normed_grad_layer(proj_grad, expanded_grad, weights, x_hat)
    expand_up, reduce_up, normed_part = add_pairs(
        [(expand_1[2], expand_sent[0]), (reduce_1[1], reduce_sent[0])],
        normed_part,
        (expand_sent[1], reduce_sent[1]),
    )
    expand_last, reduce_last = move(expand_up, False, 1), move(reduce_up, False, -1)

    places = heads // block_rows
    out_bias_grad = lax.dynamic_slice(
        grad_sum.reshape(plane, 2, block_rows),
        (column_rank % (plane // places) * places, column_rank // (plane // places), 0),
        (places, 1, block_rows),
    ).reshape(1, heads)
    attn_row = jnp.concatenate([jnp.sum(attn_bias_grad, 0), out_bias_grad], 1)
    small_grad = jnp.concatenate(
        [norm_sums.reshape(4, cols), attn_row, expand_bias_grad, jnp.zeros((10, cols), F32)], 0
    ).astype(BF)
    attn_1 = weight_grad(
        [(normed_turned, proj_grad), (grad_turned, attended)], fold(small_grad), (expand_up,)
    )
    attn_sent = ring_send(attn_1, False, -1)
    feed_2 = add_lines(
        [
            (expand_1[0], expand_sent[1], expand_last),
            (reduce_1[0], reduce_sent[1], reduce_last),
        ],
        (attn_1[0],),
    )
    feed_terms = ring_terms(feed_2)
    branch = branch_layer(
        column_rank.reshape(1).astype(jnp.int32),
        activated, attended, weights, small, attn_1[0], feed_2[0],
    )
    attn_up, branch = add_pairs(
        [(attn_1[1], attn_sent[0])], branch, (attn_sent[1], *feed_terms[1:])
    )
    attn_last = move(attn_up, False, -1)

    normed_grad = lax.psum_scatter(normed_part, COLUMN, scatter_dimension=0, tiled=True)
    branch = lax.psum_scatter(branch, COLUMN, scatter_dimension=0, tiled=True)
    input_grad = input_grad_layer(own_rows, normed_grad, small)

    yhi_index = at_yhi.reshape(1).astype(jnp.int32)
    feed_keep, send = finish_sums(yhi_index, feed_terms, 2 * cols, (attn_up,))
    feed_got = swap(send, "yhi")
    attn_2 = add_lines([(attn_1[0], attn_sent[1], attn_last)], (input_grad, feed_got))
    attn_terms = ring_terms(attn_2)
    expand_w_grad, reduce_w_grad = join_halves(
        yhi_index, feed_keep, feed_got, ((1, 0, cols), (1, cols, cols)), (attn_2[0],)
    )
    attn_keep, attn_send, small_total = finish_sums(
        yhi_index, attn_terms, cols, (expand_w_grad,)
    )
    block_out = output_layer(own_rows, branch, attn_send)
    small_total = unfold(small_total)
    norm_total = lax.dynamic_slice_in_dim(
        small_total[:4].reshape(2, width), at_plane * 8 * unit, 8 * unit, 1
    ).reshape(2, 2, 4 * unit)
    norm_keep, norm_send = pick(first_yhi, norm_total[:, 0], norm_total[:, 1])
    rider = jnp.pad(norm_send.astype(BF), ((0, 14), (0, cols - 4 * unit)))
    got = swap(jnp.concatenate([attn_send, rider], 0), "yhi")
    attn_w_grad, dense_w_grad = join_halves(
        yhi_index,
        attn_keep,
        got[:block_rows],
        ((3, 0, heads), (1, 3 * heads, heads)),
        (block_out,),
    )
    keep = norm_keep + got[block_rows : block_rows + 2, : 4 * unit].astype(F32)
    keep = keep.reshape(2, 2, 2, unit)
    keep, send = pick(first_ylo, keep[:, 0], keep[:, 1])
    keep = keep + swap(send, "ylo")
    keep, send = pick(first_core, keep[:, 0], keep[:, 1])
    norm_grads = keep + swap(send, "core")

    bias_total = lax.dynamic_slice_in_dim(
        small_total[4].reshape(4, heads), at_plane * unit, unit, 1
    )
    expand_b_grad = lax.dynamic_slice_in_dim(
        small_total[5], at_plane * expand_bias.shape[0], expand_bias.shape[0]
    )
    return (
        block_out,
        input_grad,
        norm_grads[0],
        norm_grads[1],
        attn_w_grad,
        bias_total[:3],
        dense_w_grad.T,
        bias_total[3],
        expand_w_grad,
        expand_b_grad,
        reduce_w_grad.T,
        bias_total[3],
    )


def solution(mesh):
    split = Mesh(mesh.devices.reshape(2, RING, RING, 2, 2), AXES)
    dp, tensor = ("yhi", "x", "z"), ("ylo", "core")
    rows = P(dp + tensor, None)
    vector = P(dp + tensor)
    bias = P(tensor + dp)
    parameters = (
        vector,
        vector,
        P(None, dp, tensor),
        P(None, tensor + dp),
        P(tensor, dp),
        bias,
        P(dp, tensor),
        bias,
        P(tensor, dp),
        bias,
    )
    return jax.shard_map(
        body,
        mesh=split,
        in_specs=(rows, P(dp, None)) + parameters + (rows,),
        out_specs=(rows, rows) + parameters,
        check_vma=False,
    )
```

profile of v0, /device:TPU:1, one launch (start us, length us, event | category | flops | bytes accessed | tf_op | source)
XLA Modules:
  0.0 303.3 jit_solution(6917111477838053241)
XLA Ops:
  7.2 2.1 split_columns.1
  9.4 3.8 %collective-permute-start = (bf16[64,3072]{1,0:T(8,128)(2,1)}, bf16[64,3072]{1,0:T(8,128)(2,1)S(1)}, u32[]{:S(2)}, u32[]{:S(2)}) collective-permute-start(bf16[64,3072]{1,0:T(8,128)(2,1)} %get-tuple-element.67), channel_id=1, source_target_pairs={{0,64},{64,0},{1,65},{65,1},{2,66},{66,2},{3,67},{67,3},{4,68},{68... | collective-permute-start | bytes 1179656 | tf_op jit(solution)/shard_map/ppermute | solution.py:47
  13.2 8.8 %collective-permute-done.refs_2_ = bf16[64,3072]{1,0:T(8,128)(2,1)S(1)} collective-permute-done((bf16[64,3072]{1,0:T(8,128)(2,1)}, bf16[64,3072]{1,0:T(8,128)(2,1)S(1)}, u32[]{:S(2)}, u32[]{:S(2)}) %collective-permute-start) | collective-permute-done | bytes 393248 | tf_op jit(solution)/shard_map/ppermute | solution.py:47
  24.8 2.8 collective-permute-start.11
  28.5 1.8 collective-permute-start.1
  32.1 19.0 %collective-permute-done.1 = bf16[16,1024]{1,0:T(8,128)(2,1)S(1)} collective-permute-done((bf16[16,1024]{1,0:T(8,128)(2,1)S(1)}, bf16[16,1024]{1,0:T(8,128)(2,1)S(1)}, u32[]{:S(2)}, u32[]{:S(2)}) %collective-permute-start.1) | collective-permute-done | bytes 32800 | tf_op jit(solution)/shard_map/ppermute | solution.py:47
  51.1 1.3 collective-permute-start.2
  54.5 2.4 collective-permute-start.3
  57.0 1.7 collective-permute-start.14
  58.9 1.7 collective-permute-start.4
  60.6 1.6 collective-permute-done.4
  62.2 3.7 %collective-permute-start.5 = (bf16[16,1024]{1,0:T(8,128)(2,1)S(1)}, bf16[16,1024]{1,0:T(8,128)(2,1)S(1)}, u32[]{:S(2)}, u32[]{:S(2)}) collective-permute-start(bf16[16,1024]{1,0:T(8,128)(2,1)S(1)} %add.176), channel_id=1, source_target_pairs={{0,12},{4,8},{8,4},{12,0},{1,13},{5,9},{9,5},{13,1},{2,14},{6,10},... | collective-permute-start | bytes 98312 | tf_op jit(solution)/shard_map/ppermute | solution.py:1009
  66.0 6.3 %collective-permute-start.8 = (bf16[2,128,2048]{2,1,0:T(8,128)(2,1)S(1)}, bf16[2,128,2048]{2,1,0:T(8,128)(2,1)S(1)}, u32[]{:S(2)}, u32[]{:S(2)}) collective-permute-start(bf16[2,128,2048]{2,1,0:T(8,128)(2,1)S(1)} %pair_columns.1.refs_3_.refs_0_.refs_1_), channel_id=1, source_target_pairs={{0,1},{1,0},{2,3},{3,2},{4,5},{5,4},{6,7},{7,6},{8,9},{9,8},{10,11... | collective-permute-start | bytes 3145736 | tf_op jit(solution)/shard_map/ppermute | solution.py:47
  75.3 3.1 %collective-permute-done.6 = bf16[16,1024]{1,0:T(8,128)(2,1)S(1)} collective-permute-done((bf16[16,1024]{1,0:T(8,128)(2,1)S(1)}, bf16[16,1024]{1,0:T(8,128)(2,1)S(1)}, u32[]{:S(2)}, u32[]{:S(2)}) %collective-permute-start.6) | collective-permute-done | bytes 32800 | tf_op jit(solution)/shard_map/ppermute | solution.py:47
  78.5 1.4 collective-permute-start.7
  79.9 3.2 %fusion = (f32[1024,128]{1,0:T(8,128)}, f32[1024,128]{1,0:T(8,128)}, f32[1024,128]{1,0:T(8,128)}) fusion(f32[128]{0:T(128)S(1)} %copy-done.50, f32[1024]{0:T(1024)S(1)} %subtract_convert_fusion, pred[128]{0:T(512)(128)(4,1)S(1)} %copy-done.48, pred[128]{0:T(512)(128)(4,1)S(1)} %copy-done.49, pred[128]{0:T(512)(128)(4,1)S(1)} %copy-done.51), kind=kLoop, calls=%fused_computation.3 | loop fusion | flops 655360 | bytes 1577856 | tf_op jit(solution)/shard_map/jit(_where)/select_n | solution.py:1039
  86.0 12.2 %rows.1 = (bf16[1024,2048]{1,0:T(8,128)(2,1)}, bf16[1024,2048]{1,0:T(8,128)(2,1)}, bf16[1024,2048]{1,0:T(8,128)(2,1)}, bf16[1024,2048]{1,0:T(8,128)(2,1)}, bf16[...) custom-call(s32[5]{0:T(128)} %stack.62.refs_0_, s32[16]{0:T(128)} %fusion.15.refs_1_, ...), custom_call_target="tpu_custom_call" | custom-call | bytes 29360128 | tf_op jit(solution)/shard_map/rows/pallas_call | solution.py:92
  98.1 20.2 %all-gather.2.cloned.1.call-done.refs_0_.refs_1_.refs_2_ = bf16[2048,3072]{1,0:T(8,128)(2,1)} async-done(((bf16[128,3072]{1,0:T(8,128)(2,1)}), bf16[2048,3072]{1,0:T(8,128)(2,1)}) %all-gather.2.cloned.1.call-update) | async-done | bytes 12582928 | tf_op jit(solution)/shard_map/all_gather | solution.py:992
  118.3 15.5 %expand.1 = (bf16[1024,1024]{1,0:T(8,128)(2,1)}, bf16[1024,1024]{1,0:T(8,128)(2,1)}, f32[1024,768]{1,0:T(8,128)}) custom-call(bf16[2048,3072]{1,0:T(8,128)(2,1)} %all-gather.2.cloned.1.call-done.refs_0_.refs_1_.refs_2_, bf16[2048,3072]{1,0:T(8,128)(2,1)} %all-gather.2.cloned.1.call-done.refs_0_.refs_1_.refs_2_, ...), custom_call_target="tpu_custom_call" | custom-call | flops 7516192768 | bytes 8388608 | tf_op jit(solution)/shard_map/expand/pallas_call | solution.py:92
  133.9 22.6 %feed_back.1 = (bf16[1024,1024]{1,0:T(8,128)(2,1)}, f32[1,1024]{1,0:T(1,128)}, bf16[1024,256]{1,0:T(8,128)(2,1)}, bf16[512,1024]{1,0:T(8,128)(2,1)}, bf16[512,10...) custom-call(bf16[2048,3072]{1,0:T(8,128)(2,1)} %all-gather.2.cloned., ...), custom_call_target="tpu_custom_call" | custom-call | flops 12884901888 | bytes 41943040 | tf_op jit(solution)/shard_map/feed_back/pallas_call | solution.py:92
  157.3 1.9 collective-permute-start.17
  159.2 1.3 collective-permute-start.18
  160.7 11.9 %attention.1 = (bf16[1024,256]{1,0:T(8,128)(2,1)}, bf16[1024,768]{1,0:T(8,128)(2,1)}, f32[2,1,768]{2,1,0:T(1,128)}) custom-call(f32[1024,768]{1,0:T(8,128)} %get-tuple-element.74.refs_0_, bf16[1024,256]{1,0:T(8,128)(2,1)} %get-tuple-element.78.refs_1_, f32[1024,128]{1,0:T(8,128)} %get-tuple-element.130.refs_11_.refs_2_, ...), custom_call_target="tpu_custom_call" | custom-call | flops 1879048192 | bytes 8388608 | tf_op jit(solution)/shard_map/attention/pallas_call | solution.py:92
  172.6 13.6 %normed_grad.1 = (bf16[1024,2048]{1,0:T(8,128)(2,1)}, f32[2,2048]{1,0:T(2,128)}) custom-call(bf16[2048,3072]{1,0:T(8,128)(2,1)} %all-gather.2.cloned.1.call-done.refs_0_.refs_1_.refs_2_, bf16[2048,3072]{1,0:T(8,128)(2,1)} %all-gather.2.cloned.1.call-done.refs_0_.refs_1_.refs_2_, bf16[1024,768]{1,0:T(8,128)(2,1)} %get-tuple-element.79.refs_2_, ...), custom_call_target="tpu_custom_call" | custom-call | flops 7516192768 | bytes 19398656 | tf_op jit(solution)/shard_map/normed_grad/pallas_call | solution.py:92
  188.1 3.3 %add_pairs.2 = (bf16[512,1024]{1,0:T(8,128)(2,1)}, bf16[512,1024]{1,0:T(8,128)(2,1)}, bf16[1024,2048]{1,0:T(8,128)(2,1)}) custom-call(bf16[512,1024]{1,0:T(8,128)(2,1)} %get-tuple-element.87.refs_0_, bf16[512,1024]{1,0:T(8,128)(2,1)} %bitcast.96, bf16[512,1024]{1,0:T(8,128)(2,1)} %get-tuple-element.89.refs_2_, ...), custom_call_target="tpu_custom_call", output_to_operand_aliasing={{2}: (4, {})} | custom-call | bytes 6291456 | tf_op jit(solution)/shard_map/add_pairs/pallas_call | solution.py:92
  193.8 2.5 collective-permute-start.22
  196.3 9.5 %weight_grad.1 = (bf16[512,1152]{1,0:T(8,128)(2,1)}, bf16[512,1152]{1,0:T(8,128)(2,1)}, bf16[512,1152]{1,0:T(8,128)(2,1)}, bf16[512,1152]{1,0:T(8,128)(2,1)}) custom-call(bf16[1024,2048]{1,0:T(8,128)(2,1)} %get-tuple-element.70.refs_3_.refs_0_, bf16[1024,2048]{1,0:T(8,128)(2,1)} %get-tuple-element.71.refs_5_.refs_1_, ...), custom_call_target="tpu_custom_call" | custom-call | flops 4831838208 | bytes 15466496 | tf_op jit(solution)/shard_map/weight_grad/pallas_call | solution.py:92
  205.8 2.7 collective-permute-start.20
  208.6 3.2 %collective-permute-done.21.refs_2_ = bf16[4,128,1024]{2,1,0:T(8,128)(2,1)} collective-permute-done((bf16[4,128,1024]{2,1,0:T(8,128)(2,1)}, bf16[4,128,1024]{2,1,0:T(8,128)(2,1)}, u32[]{:S(2)}, u32[]{:S(2)}) %collective-permute-start.21) | collective-permute-done | bytes 1048608 | tf_op jit(solution)/shard_map/ppermute | solution.py:34
  211.8 1.3 copy-done.2
  213.1 2.8 add_lines.2
  218.7 10.2 %branch.1.refs_2_ = bf16[1024,2048]{1,0:T(8,128)(2,1)} custom-call(s32[1]{0:T(128)} %bitcast.34.refs_0_, bf16[2048,3072]{1,0:T(8,128)(2,1)} %all-gather.2.cloned.1.call-done.refs_0_.refs_1_.refs_2_, bf16[2048,3072]{1,0:T(8,128)(2,1)} %all-gather.2.cloned.1.call-done.refs_0_.refs_1_.refs_2_, bf16[1024,1024]{1,0:T(8,128)(2,1)} %get-tuple-element.77.refs_4_.refs_3_, ...), custom_call_target="tpu_custom_call" | custom-call | flops 5368709120 | bytes 12058624 | tf_op jit(solution)/shard_map/branch/pallas_call | solution.py:92
  228.8 5.9 %collective-permute-done.24.refs_4_.refs_2_.refs_6_ = bf16[128,2048]{1,0:T(8,128)(2,1)S(1)} collective-permute-done((bf16[128,2048]{1,0:T(8,128)(2,1)}, bf16[128,2048]{1,0:T(8,128)(2,1)S(1)}, u32[]{:S(2)}, u32[]{:S(2)}) %collective-permute-start.24) | collective-permute-done | bytes 524320 | tf_op jit(solution)/shard_map/ppermute | solution.py:34
  234.7 3.4 %collective-permute-done.25.refs_5_.refs_3_.refs_7_ = bf16[128,2048]{1,0:T(8,128)(2,1)S(1)} collective-permute-done((bf16[128,2048]{1,0:T(8,128)(2,1)}, bf16[128,2048]{1,0:T(8,128)(2,1)S(1)}, u32[]{:S(2)}, u32[]{:S(2)}) %collective-permute-start.25) | collective-permute-done | bytes 524320 | tf_op jit(solution)/shard_map/ppermute | solution.py:34
  239.1 2.6 add_pairs.3
  243.2 1.3 copy-done.24
  246.2 2.7 collective-permute-start.28
  250.0 1.8 input_grad.1.refs_3_
  251.8 5.0 %collective-permute-done.28.refs_4_.refs_2_ = bf16[64,2048]{1,0:T(8,128)(2,1)} collective-permute-done((bf16[64,2048]{1,0:T(8,128)(2,1)}, bf16[64,2048]{1,0:T(8,128)(2,1)}, u32[]{:S(2)}, u32[]{:S(2)}) %collective-permute-start.28) | collective-permute-done | bytes 262176 | tf_op jit(solution)/shard_map/ppermute | solution.py:47
  258.6 2.2 add_lines.3
  261.8 1.2 collective-permute-start.30
  263.2 2.1 join_halves.2
  265.3 2.4 collective-permute-done.29.refs_2_.refs_6_.refs_10_
  267.7 4.6 %collective-permute-done.30.refs_3_.refs_7_.refs_11_ = bf16[128,1152]{1,0:T(8,128)(2,1)S(1)} collective-permute-done((bf16[128,1152]{1,0:T(8,128)(2,1)}, bf16[128,1152]{1,0:T(8,128)(2,1)S(1)}, u32[]{:S(2)}, u32[]{:S(2)}) %collective-permute-start.30) | collective-permute-done | bytes 294944 | tf_op jit(solution)/shard_map/ppermute | solution.py:34
  275.5 2.7 collective-permute-start.32
  278.3 3.0 collective-permute-done.32
  283.9 7.1 %collective-permute-start.34 = (f32[2,16]{1,0:T(2,128)S(1)}, f32[2,16]{1,0:T(2,128)S(1)}, u32[]{:S(2)}, u32[]{:S(2)}) collective-permute-start(f32[2,16]{1,0:T(2,128)S(1)} %bitcast.120), channel_id=1, source_target_pairs={{0,1},{1,0},{2,3},{3,2},{4,5},{5,4},{6,7},{7,6},{8,9},{9,8},{10,11... | collective-permute-start | bytes 392 | tf_op jit(solution)/shard_map/ppermute | solution.py:47
  294.4 1.8 join_halves.3
  (253 shorter events, 39.3 us)
Async XLA Ops:
  7.2 111.2 %all-gather.2.cloned.1.call-start = ((), (), s32[]{:S(2)}) async-start(), calls=%async_computation.2 | async-start | bytes 13369344 | tf_op jit(solution)/shard_map/all_gather | solution.py:992
  9.4 12.6 %collective-permute-start = (bf16[64,3072]{1,0:T(8,128)(2,1)}, bf16[64,3072]{1,0:T(8,128)(2,1)S(1)}, u32[]{:S(2)}, u32[]{:S(2)}) collective-permute-start(bf16[64,3072]{1,0:T(8,128)(2,1)} %get-tuple-element.67), channel_id=1, source_target_pairs={{0,64},{64,0},{1,65},{65,1},{2,66},{66,2},{3,67},{67,3},{4,68},{68... | collective-permute-start | bytes 1179656 | tf_op jit(solution)/shard_map/ppermute | solution.py:47
  24.0 224.8 %reduce-scatter.5.cloned.1.call-start = ((), (), s32[]{:S(2)}) async-start(), calls=%async_computation.4 | async-start | bytes 4718592 | tf_op jit(solution)/shard_map/reduce_scatter | solution.py:1093
  24.8 50.2 %copy-start = (bf16[2,128,2048]{2,1,0:T(8,128)(2,1)}, bf16[2,128,2048]{2,1,0:T(8,128)(2,1)S(1)}, u32[]{:S(2)}) copy-start(bf16[2,128,2048]{2,1,0:T(8,128)(2,1)S(1)} %pair_columns.1.refs_3_.refs_0_.refs_1_) | copy-start | bytes 3145732
  24.8 27.7 %collective-permute-start.11 = (bf16[2,128,2048]{2,1,0:T(8,128)(2,1)S(1)}, bf16[2,128,2048]{2,1,0:T(8,128)(2,1)S(1)}, u32[]{:S(2)}, u32[]{:S(2)}) collective-permute-start(bf16[2,128,2048]{2,1,0:T(8,128)(2,1)S(1)} %pair_columns.1.refs_3_.refs_0_.refs_1_), channel_id=1, source_target_pairs={{0,66},{2,0},{64,2},{66,64},{1,67},{3,1},{65,3},{67,65},{4,70},{6,... | collective-permute-start | bytes 3145736 | tf_op jit(solution)/shard_map/ppermute | solution.py:43
  27.6 25.0 %collective-permute-start.9 = (bf16[2,128,2048]{2,1,0:T(8,128)(2,1)S(1)}, bf16[2,128,2048]{2,1,0:T(8,128)(2,1)S(1)}, u32[]{:S(2)}, u32[]{:S(2)}) collective-permute-start(bf16[2,128,2048]{2,1,0:T(8,128)(2,1)S(1)} %pair_columns.1.refs_3_.refs_0_.refs_1_), channel_id=1, source_target_pairs={{0,2},{2,64},{64,66},{66,0},{1,3},{3,65},{65,67},{67,1},{4,6},{6,6... | collective-permute-start | bytes 3145736 | tf_op jit(solution)/shard_map/ppermute | solution.py:43
  28.5 22.6 %collective-permute-start.1 = (bf16[16,1024]{1,0:T(8,128)(2,1)S(1)}, bf16[16,1024]{1,0:T(8,128)(2,1)S(1)}, u32[]{:S(2)}, u32[]{:S(2)}) collective-permute-start(bf16[16,1024]{1,0:T(8,128)(2,1)S(1)} %dynamic_update_slice.13), channel_id=1, source_target_pairs={{0,64},{64,0},{1,65},{65,1},{2,66},{66,2},{3,67},{67,3},{4,68},{68... | collective-permute-start | bytes 98312 | tf_op jit(solution)/shard_map/ppermute | solution.py:47
  51.1 3.4 %collective-permute-start.2 = (bf16[16,1024]{1,0:T(8,128)(2,1)S(1)}, bf16[16,1024]{1,0:T(8,128)(2,1)S(1)}, u32[]{:S(2)}, u32[]{:S(2)}) collective-permute-start(bf16[16,1024]{1,0:T(8,128)(2,1)S(1)} %pad_maximum_fusion.1), channel_id=1, source_target_pairs={{0,16},{16,0},{32,48},{48,32},{1,17},{17,1},{33,49},{49,33},{2,18}... | collective-permute-start | bytes 98312 | tf_op jit(solution)/shard_map/ppermute | solution.py:1009
  52.5 22.6 %copy-start.46 = (pred[16]{0:T(512)(128)(4,1)S(1)}, pred[16]{0:T(512)(128)(4,1)}, u32[]{:S(2)}) copy-start(pred[16]{0:T(512)(128)(4,1)} %constant.186) | copy-start | bytes 52
  52.5 27.4 %copy-start.48 = (pred[128]{0:T(512)(128)(4,1)S(1)}, pred[128]{0:T(512)(128)(4,1)}, u32[]{:S(2)}) copy-start(pred[128]{0:T(512)(128)(4,1)} %constant.190) | copy-start | bytes 388
  52.5 27.4 %copy-start.49 = (pred[128]{0:T(512)(128)(4,1)S(1)}, pred[128]{0:T(512)(128)(4,1)}, u32[]{:S(2)}) copy-start(pred[128]{0:T(512)(128)(4,1)} %constant.189) | copy-start | bytes 388
  52.5 27.4 %copy-start.50 = (f32[128]{0:T(128)S(1)}, f32[128]{0:T(128)}, u32[]{:S(2)}) copy-start(f32[128]{0:T(128)} %constant.188) | copy-start | bytes 1540
  52.5 27.4 %copy-start.51 = (pred[128]{0:T(512)(128)(4,1)S(1)}, pred[128]{0:T(512)(128)(4,1)}, u32[]{:S(2)}) copy-start(pred[128]{0:T(512)(128)(4,1)} %constant.187) | copy-start | bytes 388
  52.6 22.4 %copy-start.20 = (bf16[2,128,2048]{2,1,0:T(8,128)(2,1)}, bf16[2,128,2048]{2,1,0:T(8,128)(2,1)S(1)}, u32[]{:S(2)}) copy-start(bf16[2,128,2048]{2,1,0:T(8,128)(2,1)S(1)} %collective-permute-done.11.refs_1_.refs_7_) | copy-start | bytes 3145732
  52.6 22.4 %copy-start.21 = (bf16[2,128,2048]{2,1,0:T(8,128)(2,1)}, bf16[2,128,2048]{2,1,0:T(8,128)(2,1)S(1)}, u32[]{:S(2)}) copy-start(bf16[2,128,2048]{2,1,0:T(8,128)(2,1)S(1)} %collective-permute-done.9.refs_0_.refs_5_) | copy-start | bytes 3145732
  53.6 18.6 %collective-permute-start.13 = (bf16[1,128,2048]{2,1,0:T(8,128)(2,1)}, bf16[1,128,2048]{2,1,0:T(8,128)(2,1)}, u32[]{:S(2)}, u32[]{:S(2)}) collective-permute-start(bf16[1,128,2048]{2,1,0:T(8,128)(2,1)} %get-tuple-element.68), channel_id=1, source_target_pairs={{0,2},{2,64},{64,66},{66,0},{1,3},{3,65},{65,67},{67,1},{4,6},{6,6... | collective-permute-start | bytes 1572872 | tf_op jit(solution)/shard_map/ppermute | solution.py:43
  54.5 4.3 %collective-permute-start.3 = (bf16[16,1024]{1,0:T(8,128)(2,1)S(1)}, bf16[16,1024]{1,0:T(8,128)(2,1)S(1)}, u32[]{:S(2)}, u32[]{:S(2)}) collective-permute-start(bf16[16,1024]{1,0:T(8,128)(2,1)S(1)} %fusion.20), channel_id=1, source_target_pairs={{0,48},{16,32},{32,16},{48,0},{1,49},{17,33},{33,17},{49,1},{2,50}... | collective-permute-start | bytes 98312 | tf_op jit(solution)/shard_map/ppermute | solution.py:1009
  57.0 16.9 %collective-permute-start.14 = (bf16[1,128,2048]{2,1,0:T(8,128)(2,1)}, bf16[1,128,2048]{2,1,0:T(8,128)(2,1)}, u32[]{:S(2)}, u32[]{:S(2)}) collective-permute-start(bf16[1,128,2048]{2,1,0:T(8,128)(2,1)} %get-tuple-element.69), channel_id=1, source_target_pairs={{0,66},{2,0},{64,2},{66,64},{1,67},{3,1},{65,3},{67,65},{4,70},{6,... | collective-permute-start | bytes 1572872 | tf_op jit(solution)/shard_map/ppermute | solution.py:43
  58.9 3.4 %collective-permute-start.4 = (bf16[16,1024]{1,0:T(8,128)(2,1)S(1)}, bf16[16,1024]{1,0:T(8,128)(2,1)S(1)}, u32[]{:S(2)}, u32[]{:S(2)}) collective-permute-start(bf16[16,1024]{1,0:T(8,128)(2,1)S(1)} %add.175), channel_id=1, source_target_pairs={{0,4},{4,0},{8,12},{12,8},{1,5},{5,1},{9,13},{13,9},{2,6},{6,2},{1... | collective-permute-start | bytes 98312 | tf_op jit(solution)/shard_map/ppermute | solution.py:1009
  62.2 12.9 %collective-permute-start.5 = (bf16[16,1024]{1,0:T(8,128)(2,1)S(1)}, bf16[16,1024]{1,0:T(8,128)(2,1)S(1)}, u32[]{:S(2)}, u32[]{:S(2)}) collective-permute-start(bf16[16,1024]{1,0:T(8,128)(2,1)S(1)} %add.176), channel_id=1, source_target_pairs={{0,12},{4,8},{8,4},{12,0},{1,13},{5,9},{9,5},{13,1},{2,14},{6,10},... | collective-permute-start | bytes 98312 | tf_op jit(solution)/shard_map/ppermute | solution.py:1009
  66.0 17.8 %collective-permute-start.8 = (bf16[2,128,2048]{2,1,0:T(8,128)(2,1)S(1)}, bf16[2,128,2048]{2,1,0:T(8,128)(2,1)S(1)}, u32[]{:S(2)}, u32[]{:S(2)}) collective-permute-start(bf16[2,128,2048]{2,1,0:T(8,128)(2,1)S(1)} %pair_columns.1.refs_3_.refs_0_.refs_1_), channel_id=1, source_target_pairs={{0,1},{1,0},{2,3},{3,2},{4,5},{5,4},{6,7},{7,6},{8,9},{9,8},{10,11... | collective-permute-start | bytes 3145736 | tf_op jit(solution)/shard_map/ppermute | solution.py:47
  72.3 11.5 %collective-permute-start.12 = (bf16[2,128,2048]{2,1,0:T(8,128)(2,1)S(1)}, bf16[2,128,2048]{2,1,0:T(8,128)(2,1)S(1)}, u32[]{:S(2)}, u32[]{:S(2)}) collective-permute-start(bf16[2,128,2048]{2,1,0:T(8,128)(2,1)S(1)} %collective-permute-done.11.refs_1_.refs_7_), channel_id=1, source_target_pairs={{0,1},{1,0},{2,3},{3,2},{4,5},{5,4},{6,7},{7,6},{8,9},{9,8},{10,11... | collective-permute-start | bytes 3145736 | tf_op jit(solution)/shard_map/ppermute | solution.py:47
  72.3 11.5 %collective-permute-start.10 = (bf16[2,128,2048]{2,1,0:T(8,128)(2,1)S(1)}, bf16[2,128,2048]{2,1,0:T(8,128)(2,1)S(1)}, u32[]{:S(2)}, u32[]{:S(2)}) collective-permute-start(bf16[2,128,2048]{2,1,0:T(8,128)(2,1)S(1)} %collective-permute-done.9.refs_0_.refs_5_), channel_id=1, source_target_pairs={{0,1},{1,0},{2,3},{3,2},{4,5},{5,4},{6,7},{7,6},{8,9},{9,8},{10,11... | collective-permute-start | bytes 3145736 | tf_op jit(solution)/shard_map/ppermute | solution.py:47
  75.0 8.8 %collective-permute-start.15 = (bf16[2,128,2048]{2,1,0:T(8,128)(2,1)S(1)}, bf16[2,128,2048]{2,1,0:T(8,128)(2,1)S(1)}, u32[]{:S(2)}, u32[]{:S(2)}) collective-permute-start(bf16[2,128,2048]{2,1,0:T(8,128)(2,1)S(1)} %constant_dynamic-update-slice_fusion.refs_9_), channel_id=1, source_target_pairs={{0,1},{1,0},{2,3},{3,2},{4,5},{5,4},{6,7},{7,6},{8,9},{9,8},{10,11... | collective-permute-start | bytes 3145736 | tf_op jit(solution)/shard_map/ppermute | solution.py:47
  75.2 3.2 %collective-permute-start.6 = (bf16[16,1024]{1,0:T(8,128)(2,1)S(1)}, bf16[16,1024]{1,0:T(8,128)(2,1)S(1)}, u32[]{:S(2)}, u32[]{:S(2)}) collective-permute-start(bf16[16,1024]{1,0:T(8,128)(2,1)S(1)} %get-tuple-element.122), channel_id=1, source_target_pairs={{0,2},{2,0},{1,3},{3,1},{4,6},{6,4},{5,7},{7,5},{8,10},{10,8},{9,1... | collective-permute-start | bytes 98312 | tf_op jit(solution)/shard_map/ppermute | solution.py:47
  78.5 4.6 %collective-permute-start.7 = (bf16[16,1024]{1,0:T(8,128)(2,1)S(1)}, bf16[16,1024]{1,0:T(8,128)(2,1)S(1)}, u32[]{:S(2)}, u32[]{:S(2)}) collective-permute-start(bf16[16,1024]{1,0:T(8,128)(2,1)S(1)} %fusion.19), channel_id=1, source_target_pairs={{0,1},{1,0},{2,3},{3,2},{4,5},{5,4},{6,7},{7,6},{8,9},{9,8},{10,11... | collective-permute-start | bytes 98312 | tf_op jit(solution)/shard_map/ppermute | solution.py:47
  156.4 29.7 %collective-permute-start.16 = (bf16[4,128,1024]{2,1,0:T(8,128)(2,1)}, bf16[4,128,1024]{2,1,0:T(8,128)(2,1)S(1)}, u32[]{:S(2)}, u32[]{:S(2)}) collective-permute-start(bf16[4,128,1024]{2,1,0:T(8,128)(2,1)} %bitcast.128), channel_id=1, source_target_pairs={{0,4},{1,17},{4,8},{5,21},{8,12},{9,25},{12,0},{13,29},{16,20},{17... | collective-permute-start | bytes 3145736 | tf_op jit(solution)/shard_map/ppermute | solution.py:34
  157.3 28.8 %collective-permute-start.17 = (bf16[4,128,1024]{2,1,0:T(8,128)(2,1)}, bf16[4,128,1024]{2,1,0:T(8,128)(2,1)S(1)}, u32[]{:S(2)}, u32[]{:S(2)}) collective-permute-start(bf16[4,128,1024]{2,1,0:T(8,128)(2,1)} %bitcast.127), channel_id=1, source_target_pairs={{0,12},{1,49},{4,0},{5,53},{8,4},{9,57},{12,8},{13,61},{16,28},{17... | collective-permute-start | bytes 3145736 | tf_op jit(solution)/shard_map/ppermute | solution.py:34
  159.2 26.9 %collective-permute-start.18 = (bf16[4,128,1024]{2,1,0:T(8,128)(2,1)}, bf16[4,128,1024]{2,1,0:T(8,128)(2,1)S(1)}, u32[]{:S(2)}, u32[]{:S(2)}) collective-permute-start(bf16[4,128,1024]{2,1,0:T(8,128)(2,1)} %bitcast.126), channel_id=1, source_target_pairs={{0,12},{1,49},{4,0},{5,53},{8,4},{9,57},{12,8},{13,61},{16,28},{17... | collective-permute-start | bytes 3145736 | tf_op jit(solution)/shard_map/ppermute | solution.py:34
  160.5 25.7 %collective-permute-start.19 = (bf16[4,128,1024]{2,1,0:T(8,128)(2,1)}, bf16[4,128,1024]{2,1,0:T(8,128)(2,1)S(1)}, u32[]{:S(2)}, u32[]{:S(2)}) collective-permute-start(bf16[4,128,1024]{2,1,0:T(8,128)(2,1)} %bitcast.125), channel_id=1, source_target_pairs={{0,4},{1,17},{4,8},{5,21},{8,12},{9,25},{12,0},{13,29},{16,20},{17... | collective-permute-start | bytes 3145736 | tf_op jit(solution)/shard_map/ppermute | solution.py:34
  191.4 100.9 %reduce-scatter.3.cloned.1.call-start = ((), (), s32[]{:S(2)}) async-start(), calls=%async_computation.3 | async-start | bytes 4718592 | tf_op jit(solution)/shard_map/reduce_scatter | solution.py:1094
  193.8 14.8 %collective-permute-start.22 = (bf16[4,128,1024]{2,1,0:T(8,128)(2,1)}, bf16[4,128,1024]{2,1,0:T(8,128)(2,1)}, u32[]{:S(2)}, u32[]{:S(2)}) collective-permute-start(bf16[4,128,1024]{2,1,0:T(8,128)(2,1)} %bitcast.38), channel_id=1, source_target_pairs={{0,12},{1,49},{4,0},{5,53},{8,4},{9,57},{12,8},{13,61},{16,28},{17... | collective-permute-start | bytes 3145736 | tf_op jit(solution)/shard_map/ppermute | solution.py:34
  196.3 15.5 %collective-permute-start.21 = (bf16[4,128,1024]{2,1,0:T(8,128)(2,1)}, bf16[4,128,1024]{2,1,0:T(8,128)(2,1)}, u32[]{:S(2)}, u32[]{:S(2)}) collective-permute-start(bf16[4,128,1024]{2,1,0:T(8,128)(2,1)} %bitcast.31.refs_5_), channel_id=1, source_target_pairs={{0,4},{1,17},{4,8},{5,21},{8,12},{9,25},{12,0},{13,29},{16,20},{17... | collective-permute-start | bytes 3145736 | tf_op jit(solution)/shard_map/ppermute | solution.py:34
  196.3 15.5 %copy-start.26 = (bf16[512,1024]{1,0:T(8,128)(2,1)S(1)}, bf16[512,1024]{1,0:T(8,128)(2,1)}, u32[]{:S(2)}) copy-start(bf16[512,1024]{1,0:T(8,128)(2,1)} %get-tuple-element.99) | copy-start | bytes 3145732
  205.8 23.0 %collective-permute-start.20 = (bf16[4,128,1152]{2,1,0:T(8,128)(2,1)}, bf16[4,128,1152]{2,1,0:T(8,128)(2,1)}, u32[]{:S(2)}, u32[]{:S(2)}) collective-permute-start(bf16[4,128,1152]{2,1,0:T(8,128)(2,1)} %bitcast.124), channel_id=1, source_target_pairs={{0,12},{1,49},{4,0},{5,53},{8,4},{9,57},{12,8},{13,61},{16,28},{17... | collective-permute-start | bytes 3538952 | tf_op jit(solution)/shard_map/ppermute | solution.py:34
  208.6 20.3 %collective-permute-start.23 = (bf16[4,128,1152]{2,1,0:T(8,128)(2,1)}, bf16[4,128,1152]{2,1,0:T(8,128)(2,1)S(1)}, u32[]{:S(2)}, u32[]{:S(2)}) collective-permute-start(bf16[4,128,1152]{2,1,0:T(8,128)(2,1)} %bitcast.123), channel_id=1, source_target_pairs={{0,4},{1,17},{4,8},{5,21},{8,12},{9,25},{12,0},{13,29},{16,20},{17... | collective-permute-start | bytes 3538952 | tf_op jit(solution)/shard_map/ppermute | solution.py:34
  216.7 18.0 %collective-permute-start.24 = (bf16[128,2048]{1,0:T(8,128)(2,1)}, bf16[128,2048]{1,0:T(8,128)(2,1)S(1)}, u32[]{:S(2)}, u32[]{:S(2)}) collective-permute-start(bf16[128,2048]{1,0:T(8,128)(2,1)} %get-tuple-element.103), channel_id=1, source_target_pairs={{0,48},{1,13},{4,52},{5,1},{8,56},{9,5},{12,60},{13,9},{16,0},{17,... | collective-permute-start | bytes 1572872 | tf_op jit(solution)/shard_map/ppermute | solution.py:34
  217.1 21.0 %collective-permute-start.25 = (bf16[128,2048]{1,0:T(8,128)(2,1)}, bf16[128,2048]{1,0:T(8,128)(2,1)S(1)}, u32[]{:S(2)}, u32[]{:S(2)}) collective-permute-start(bf16[128,2048]{1,0:T(8,128)(2,1)} %get-tuple-element.104), channel_id=1, source_target_pairs={{0,16},{1,5},{4,20},{5,9},{8,24},{9,13},{12,28},{13,1},{16,32},{17... | collective-permute-start | bytes 1572872 | tf_op jit(solution)/shard_map/ppermute | solution.py:34
  218.2 20.0 %collective-permute-start.26 = (bf16[128,2048]{1,0:T(8,128)(2,1)S(1)}, bf16[128,2048]{1,0:T(8,128)(2,1)S(1)}, u32[]{:S(2)}, u32[]{:S(2)}) collective-permute-start(bf16[128,2048]{1,0:T(8,128)(2,1)S(1)} %get-tuple-element.105), channel_id=1, source_target_pairs={{0,32},{1,9},{4,36},{5,13},{8,40},{9,1},{12,44},{13,5},{16,48},{17... | collective-permute-start | bytes 1572872 | tf_op jit(solution)/shard_map/ppermute | solution.py:34
  241.8 15.7 %collective-permute-start.27 = (bf16[4,128,1152]{2,1,0:T(8,128)(2,1)}, bf16[4,128,1152]{2,1,0:T(8,128)(2,1)}, u32[]{:S(2)}, u32[]{:S(2)}) collective-permute-start(bf16[4,128,1152]{2,1,0:T(8,128)(2,1)} %bitcast.91), channel_id=1, source_target_pairs={{0,12},{1,49},{4,0},{5,53},{8,4},{9,57},{12,8},{13,61},{16,28},{17... | collective-permute-start | bytes 3538952 | tf_op jit(solution)/shard_map/ppermute | solution.py:34
  246.2 10.7 %collective-permute-start.28 = (bf16[64,2048]{1,0:T(8,128)(2,1)}, bf16[64,2048]{1,0:T(8,128)(2,1)}, u32[]{:S(2)}, u32[]{:S(2)}) collective-permute-start(bf16[64,2048]{1,0:T(8,128)(2,1)} %get-tuple-element.109), channel_id=1, source_target_pairs={{0,64},{64,0},{1,65},{65,1},{2,66},{66,2},{3,67},{67,3},{4,68},{68... | collective-permute-start | bytes 786440 | tf_op jit(solution)/shard_map/ppermute | solution.py:47
  261.5 6.2 %collective-permute-start.29 = (bf16[128,1152]{1,0:T(8,128)(2,1)}, bf16[128,1152]{1,0:T(8,128)(2,1)S(1)}, u32[]{:S(2)}, u32[]{:S(2)}) collective-permute-start(bf16[128,1152]{1,0:T(8,128)(2,1)} %get-tuple-element.111), channel_id=1, source_target_pairs={{0,48},{1,13},{4,52},{5,1},{8,56},{9,5},{12,60},{13,9},{16,0},{17,... | collective-permute-start | bytes 884744 | tf_op jit(solution)/shard_map/ppermute | solution.py:34
  261.8 10.6 %collective-permute-start.30 = (bf16[128,1152]{1,0:T(8,128)(2,1)}, bf16[128,1152]{1,0:T(8,128)(2,1)S(1)}, u32[]{:S(2)}, u32[]{:S(2)}) collective-permute-start(bf16[128,1152]{1,0:T(8,128)(2,1)} %get-tuple-element.112), channel_id=1, source_target_pairs={{0,16},{1,5},{4,20},{5,9},{8,24},{9,13},{12,28},{13,1},{16,32},{17... | collective-permute-start | bytes 884744 | tf_op jit(solution)/shard_map/ppermute | solution.py:34
  263.0 9.4 %collective-permute-start.31 = (bf16[128,1152]{1,0:T(8,128)(2,1)}, bf16[128,1152]{1,0:T(8,128)(2,1)S(1)}, u32[]{:S(2)}, u32[]{:S(2)}) collective-permute-start(bf16[128,1152]{1,0:T(8,128)(2,1)} %get-tuple-element.113), channel_id=1, source_target_pairs={{0,32},{1,9},{4,36},{5,13},{8,40},{9,1},{12,44},{13,5},{16,48},{17... | collective-permute-start | bytes 884744 | tf_op jit(solution)/shard_map/ppermute | solution.py:34
  275.5 5.9 %collective-permute-start.32 = (bf16[80,1024]{1,0:T(8,128)(2,1)S(1)}, bf16[80,1024]{1,0:T(8,128)(2,1)S(1)}, u32[]{:S(2)}, u32[]{:S(2)}) collective-permute-start(bf16[80,1024]{1,0:T(8,128)(2,1)S(1)} %fusion.5), channel_id=1, source_target_pairs={{0,64},{64,0},{1,65},{65,1},{2,66},{66,2},{3,67},{67,3},{4,68},{68... | collective-permute-start | bytes 491528 | tf_op jit(solution)/shard_map/ppermute | solution.py:47
  278.3 18.4 %copy-start.47 = (f32[4,16]{1,0:T(4,128)}, f32[4,16]{1,0:T(4,128)S(1)}, u32[]{:S(2)}) copy-start(f32[4,16]{1,0:T(4,128)S(1)} %constant_dynamic-slice_fusion) | copy-start | bytes 772
  281.4 2.5 collective-permute-start.33
  283.9 7.9 %collective-permute-start.34 = (f32[2,16]{1,0:T(2,128)S(1)}, f32[2,16]{1,0:T(2,128)S(1)}, u32[]{:S(2)}, u32[]{:S(2)}) collective-permute-start(f32[2,16]{1,0:T(2,128)S(1)} %bitcast.120), channel_id=1, source_target_pairs={{0,1},{1,0},{2,3},{3,2},{4,5},{5,4},{6,7},{7,6},{8,9},{9,8},{10,11... | collective-permute-start | bytes 392 | tf_op jit(solution)/shard_map/ppermute | solution.py:47
  (51 other events, 270.9 us)
Sparse Core Ops, SparseCore 0:
  24.2 94.1 all-gather.1
  191.6 35.4 reduce-scatter.4
  241.9 38.4 reduce-scatter.2
where the time goes:
time: 304 us; the launch traced here: 303 us
  Pallas kernels  118 us (39%)
  waiting for transfers between devices  83 us (27%)
  starting transfers between devices  54.7 us (18%)
  local copies, waits for them, and re-layouts  24.6 us (8%)
  between operations  14.6 us (5%)
  other arithmetic  8.57 us (3%)
    pallas_call x19, Pallas kernels, kernel_call(): return pl.pallas_call(run, **options)(*operands, *waits)  116 us
    ppermute x12, waiting for transfers between devices, swap(): return lax.ppermute(value, axis, [(0, 1), (1, 0)])  40 us
    ppermute x12, starting transfers between devices, swap(): return lax.ppermute(value, axis, [(0, 1), (1, 0)])  27.6 us
    ppermute x15, waiting for transfers between devices, move(): return lax.ppermute(value, ('x', 'z', 'core'), ring_pairs(first_ring, step))  20.2 us
    all_gather x1, waiting for transfers between devices, body(): weights = lax.all_gather(block, ('x', 'z'), axis=0, tiled=True)  20.2 us
    unnamed x129, local copies, waits for them, and re-layouts  17.6 us
    ppermute x15, starting transfers between devices, move(): return lax.ppermute(value, ('x', 'z', 'core'), ring_pairs(first_ring, step))  13.4 us
    ppermute x4, starting transfers between devices, body(): small = small + lax.ppermute(small, axis, axis_swaps(odd))  9.08 us
  transfers between devices with their start and end apart: 38, of which 16 were waited for; matrix products, arithmetic and copies ran while one was open for 5% of the time, Pallas kernels for 24%

commit v1 on v0

--- a/solution.py
+++ b/solution.py
@@ -142,33 +142,40 @@
     return [total.reshape(shape) for total, shape in zip(sums, shapes)] + [carried]
 
 
-def add_lines_kernel(*refs):
+def add_lines_kernel(riders, *refs):
     outs = refs[-RING:]
-    sources, at = refs[:-RING], 0
+    sources, at = refs[: -RING - riders], 0
     for n in range(0, len(sources), 3):
         total = sum(ref[...].astype(F32) for ref in sources[n : n + 3])
         for i, out in enumerate(outs):
             out[:, at : at + total.shape[-1]] = total[i].astype(BF)
         at += total.shape[-1]
-
-
-def add_lines(lines, waits=()):
+    for ref in refs[len(sources) : -RING]:
+        for out in outs:
+            out[:, at:] = ref[...]
+
+
+def add_lines(lines, riders=(), waits=()):
     operands = [term for terms in lines for term in terms]
     rows = operands[0].shape[1]
-    cols = sum(terms[0].shape[2] for terms in lines)
+    cols = sum(terms[0].shape[2] for terms in lines) + sum(rider.shape[1] for rider in riders)
     at_once = rows // 2
+
+    def kernel(*refs):
+        add_lines_kernel(len(riders), *refs)
+
     specs = [
         pl.BlockSpec((RING, at_once, term.shape[2]), lambda i: (0, i, 0)) for term in operands
     ]
     return kernel_call(
-        add_lines_kernel,
-        tuple(operands),
+        kernel,
+        (*operands, *riders),
         waits,
         grid=(2,),
-        in_specs=specs,
+        in_specs=specs + [row_block(at_once, rider.shape[1]) for rider in riders],
         out_specs=(row_block(at_once, cols),) * RING,
         out_shape=(shaped((rows, cols), BF),) * RING,
-        compiler_params=params(SMALL),
+        compiler_params=params(BIG),
         cost_estimate=cost(0, 8 * RING * rows * cols),
         name="add_lines",
     )
@@ -528,7 +535,10 @@
     )
 
 
-def expand_kernel(weight, qkv_w, normed, small, activated, slope, projected):
+def expand_kernel(
+    weight, qkv_w, dense_w, normed, grad, small, activated, slope, projected, attended_grad
+):
+    attended_grad[...] = dot_nn(grad[...], dense_w[...]).astype(BF)
     projected[...] = dot_nn(normed[...], qkv_w[...]) + small[12:13, : projected.shape[1]]
     u = dot_nn(normed[...], weight[...]) + small[14:15]
     factor = (2.0 / np.pi) ** 0.5
@@ -540,24 +550,27 @@
     slope[...] = (half + 0.5 * u * (1.0 - bent * bent) * rise).astype(BF)
 
 
-def expand_layer(weights, normed, small, *waits):
+def expand_layer(weights, normed, grad, small, *waits):
     rows, width = normed.shape
-    cols = weights.shape[1] // 3
+    cols = weights.shape[1] // 2
     three = cols // 4 * 3
     at_once = 256
     return kernel_call(
         expand_kernel,
-        (weights, weights, normed, small),
+        (weights, weights, weights, normed, grad, small),
         waits,
         grid=(rows // at_once,),
         in_specs=[
             pl.BlockSpec((width, cols), lambda i: (0, 1)),
             pl.BlockSpec((width, three), lambda i: (0, 0)),
+            pl.BlockSpec((width, cols // 4), lambda i: (0, 3)),
+            row_block(at_once, width),
             row_block(at_once, width),
             whole(small.shape),
         ],
-        out_specs=(row_block(at_once, cols),) * 2 + (row_block(at_once, three),),
-        out_shape=(shaped((rows, cols), BF),) * 2 + (shaped((rows, three), F32),),
+        out_specs=(row_block(at_once, cols),) * 2 + (row_block(at_once, three), row_block(at_once, cols // 4)),
+        out_shape=(shaped((rows, cols), BF),) * 2
+        + (shaped((rows, three), F32), shaped((rows, cols // 4), BF)),
         compiler_params=params(BIG),
         cost_estimate=cost(2 * rows * width * (cols + three), 4 * rows * width, rows * cols),
         name="expand",
@@ -565,9 +578,9 @@
 
 
 def feed_back_kernel(weights, grad, slope, normed, activated, grad_turned, *refs):
-    eg_out, bias_grad, attended_grad, *outs = refs[: 3 + 2 * RING]
-    weight_v, dense_v, grad_v, slope_v, normed_v, activated_v, turned_v, eg_v, hold, *rest = refs[
-        3 + 2 * RING :
+    eg_out, bias_grad, *outs = refs[: 2 + 2 * RING]
+    weight_v, grad_v, slope_v, normed_v, activated_v, turned_v, eg_v, hold, *rest = refs[
+        2 + 2 * RING :
     ]
     sems, out_sems = rest
     step = pl.program_id(0)
@@ -575,13 +588,11 @@
     quarter = grad.shape[1] // RING
 
     def loads():
-        cols = weight_v.shape[1]
-        made = [(weights.at[:, pl.ds(2 * cols, cols)], weight_v)]
+        made = [(weights, weight_v)]
         for n in range(RING):
             made.append((grad.at[pl.ds(n * tile, tile)], grad_v.at[pl.ds(n * tile, tile)]))
         made += [
             (slope, slope_v), (normed, normed_v), (activated, activated_v), (grad_turned, turned_v),
-            (weights.at[:, pl.ds(cols - dense_v.shape[1], dense_v.shape[1])], dense_v),
         ]
         return [pltpu.make_async_copy(a, b, sems.at[n]) for n, (a, b) in enumerate(made)]
 
@@ -592,11 +603,10 @@
     @pl.when(step == 0)
     def _():
         copies = loads()
-        for n in (0, 1, 5, 9, 2, 3, 4, 6, 7, 8):
+        for n in (0, 1, 5, 2, 3, 4, 6, 7, 8):
             copies[n].start()
         copies[0].wait()
         copies[5].wait()
-        copies[9].wait()
         bias_grad[...] = jnp.zeros_like(bias_grad)
 
     for n in range(RING):
@@ -611,7 +621,6 @@
         low = dot_nn(grad_v[at, :], weight_v[...]) * slope_v[at, :].astype(F32)
         low = low.astype(BF)
         eg_v[at, :] = low
-        attended_grad[at, :] = dot_nn(grad_v[at, :], dense_v[...]).astype(BF)
         bias_grad[...] += jnp.sum(low.astype(F32), 0, keepdims=True)
 
     @pl.when(step == RING)
@@ -649,7 +658,7 @@
 
 def feed_back(weights, grad, slope, normed, activated, grad_turned, *waits):
     rows, width = grad.shape
-    cols = weights.shape[1] // 3
+    cols = weights.shape[1]
     depth = width // RING
     outs = kernel_call(
         feed_back_kernel,
@@ -657,12 +666,11 @@
         waits,
         grid=(3 * RING,),
         in_specs=[ANY] * 6,
-        out_specs=(ANY, whole((1, cols)), whole((rows, cols // 4))) + (ANY,) * (2 * RING),
-        out_shape=(shaped((rows, cols), BF), shaped((1, cols), F32), shaped((rows, cols // 4), BF))
+        out_specs=(ANY, whole((1, cols))) + (ANY,) * (2 * RING),
+        out_shape=(shaped((rows, cols), BF), shaped((1, cols), F32))
         + (shaped((depth, cols), BF),) * (2 * RING),
         scratch_shapes=[
             pltpu.VMEM((width, cols), BF),
-            pltpu.VMEM((width, cols // 4), BF),
             pltpu.VMEM((rows, width), BF),
             pltpu.VMEM((rows, cols), BF),
             pltpu.VMEM((rows, width), BF),
@@ -670,15 +678,15 @@
             pltpu.VMEM((rows, width), BF),
             pltpu.VMEM((rows, cols), BF),
             pltpu.VMEM((2 * RING, depth, cols), BF),
-            pltpu.SemaphoreType.DMA((RING + 6,)),
+            pltpu.SemaphoreType.DMA((RING + 5,)),
             pltpu.SemaphoreType.DMA((2 * RING + 1,)),
         ],
         compiler_params=params(BIG),
         cost_estimate=cost(6 * rows * width * cols, 20 * rows * width),
         name="feed_back",
     )
-    quarters = [quarter.reshape(RING, -1, cols) for quarter in outs[3:]]
-    return *outs[:3], quarters[:RING], quarters[RING:]
+    quarters = [quarter.reshape(RING, -1, cols) for quarter in outs[2:]]
+    return *outs[:2], quarters[:RING], quarters[RING:]
 
 
 def branch_kernel(rank, dense, reduce, activated, attended, small, branch, bias):
@@ -701,19 +709,19 @@
     branch[...] = (total + bias[...]).astype(BF)
 
 
-def branch_layer(rank, activated, attended, weights, small, *waits):
+def branch_layer(rank, activated, attended, weights, reduce_w, small, *waits):
     rows, cols = activated.shape
     heads = attended.shape[1]
     width = weights.shape[0]
     at_once = 256
     return kernel_call(
         branch_kernel,
-        (rank, weights, weights, activated, attended, small),
+        (rank, weights, reduce_w, activated, attended, small),
         waits,
         grid=(rows // at_once,),
         in_specs=[SMEM]
         + [pl.BlockSpec((width, heads), lambda i: (0, 3))]
-        + [pl.BlockSpec((width, cols), lambda i: (0, 2))]
+        + [whole((width, cols))]
         + [row_block(at_once, cols), row_block(at_once, heads), whole(small.shape)],
         out_specs=row_block(at_once, width),
         out_shape=shaped((rows, width), BF),
@@ -989,7 +997,8 @@
     )
     got = swap(other, "yhi")
     block = jnp.concatenate(pick(first_yhi, own, got), 0)
-    weights = lax.all_gather(block, ("x", "z"), axis=0, tiled=True)
+    weights = lax.all_gather(block[:, : 2 * cols], ("x", "z"), axis=0, tiled=True)
+    reduce_w = lax.all_gather(block[:, 2 * cols :], ("x", "z"), axis=0, tiled=True)
 
     small = small + swap(small, "yhi")
     two = small[15, : 4 * count].astype(F32).reshape(2, 2, count)
@@ -1042,16 +1051,26 @@
     normed, normed_turned, x_hat, grad_all, grad_turned, grad_sum = rows_layer(
         chips, turned, small, sources, cos, sin_low, sin_high, start
     )
-    activated, slope, projected = expand_layer(weights, normed, small)
-    expanded_grad, expand_bias_grad, attended_grad, expand_1, reduce_1 = feed_back(
-        weights, grad_all, slope, normed_turned, activated, grad_turned
+    activated, slope, projected, attended_grad = expand_layer(weights, normed, grad_all, small)
+    attended, proj_grad, attn_bias_grad = attention(
+        projected, attended_grad, cos, sin_low, sin_high, start, pack_rows
+    )
+    attn_1 = weight_grad([(normed_turned, proj_grad), (grad_turned, attended)])
+    attn_sent = ring_send(attn_1, False, -1)
+    branch = branch_layer(
+        column_rank.reshape(1).astype(jnp.int32),
+        activated, attended, weights, reduce_w, small, attn_1[0],
+    )
+    attn_up, branch = add_pairs([(attn_1[1], attn_sent[0])], branch, (attn_sent[1],))
+    attn_last = move(attn_up, False, -1)
+    expanded_grad, expand_bias_grad, expand_1, reduce_1 = feed_back(
+        reduce_w, grad_all, slope, normed_turned, activated, grad_turned, attn_up
     )
     expand_sent = ring_send(expand_1, False, 1)
     reduce_sent = ring_send(reduce_1, False, -1)
-    attended, proj_grad, attn_bias_grad = attention(
-        projected, attended_grad, cos, sin_low, sin_high, start, pack_rows
-    )
-    normed_part, norm_sums = normed_grad_layer(proj_grad, expanded_grad, weights, x_hat)
+    normed_part, norm_sums = normed_grad_layer(
+        proj_grad, expanded_grad, weights, x_hat, expand_1[0], attn_last
+    )
     expand_up, reduce_up, normed_part = add_pairs(
         [(expand_1[2], expand_sent[0]), (reduce_1[1], reduce_sent[0])],
         normed_part,
@@ -1066,59 +1085,51 @@
         (places, 1, block_rows),
     ).reshape(1, heads)
     attn_row = jnp.concatenate([jnp.sum(attn_bias_grad, 0), out_bias_grad], 1)
-    small_grad = jnp.concatenate(
+    small_sums = jnp.concatenate(
         [norm_sums.reshape(4, cols), attn_row, expand_bias_grad, jnp.zeros((10, cols), F32)], 0
-    ).astype(BF)
-    attn_1 = weight_grad(
-        [(normed_turned, proj_grad), (grad_turned, attended)], fold(small_grad), (expand_up,)
-    )
-    attn_sent = ring_send(attn_1, False, -1)
+    )
+    small_sums = sum((move(small_sums, False, step) for step in (1, 2, 3)), small_sums)
+
+    branch = lax.psum_scatter(branch, COLUMN, scatter_dimension=0, tiled=True)
+    normed_grad = lax.psum_scatter(normed_part, COLUMN, scatter_dimension=0, tiled=True)
+    block_out = output_layer(own_rows, branch, expand_up)
+
+    yhi_index = at_yhi.reshape(1).astype(jnp.int32)
     feed_2 = add_lines(
         [
             (expand_1[0], expand_sent[1], expand_last),
             (reduce_1[0], reduce_sent[1], reduce_last),
         ],
-        (attn_1[0],),
+        [fold(small_sums).astype(BF)],
     )
     feed_terms = ring_terms(feed_2)
-    branch = branch_layer(
-        column_rank.reshape(1).astype(jnp.int32),
-        activated, attended, weights, small, attn_1[0], feed_2[0],
-    )
-    attn_up, branch = add_pairs(
-        [(attn_1[1], attn_sent[0])], branch, (attn_sent[1], *feed_terms[1:])
-    )
-    attn_last = move(attn_up, False, -1)
-
-    normed_grad = lax.psum_scatter(normed_part, COLUMN, scatter_dimension=0, tiled=True)
-    branch = lax.psum_scatter(branch, COLUMN, scatter_dimension=0, tiled=True)
-    input_grad = input_grad_layer(own_rows, normed_grad, small)
-
-    yhi_index = at_yhi.reshape(1).astype(jnp.int32)
-    feed_keep, send = finish_sums(yhi_index, feed_terms, 2 * cols, (attn_up,))
-    feed_got = swap(send, "yhi")
-    attn_2 = add_lines([(attn_1[0], attn_sent[1], attn_last)], (input_grad, feed_got))
+    attn_2 = add_lines([(attn_1[0], attn_sent[1], attn_last)], waits=(feed_2[0],))
+    input_grad = input_grad_layer(own_rows, normed_grad, small, attn_2[0])
     attn_terms = ring_terms(attn_2)
-    expand_w_grad, reduce_w_grad = join_halves(
-        yhi_index, feed_keep, feed_got, ((1, 0, cols), (1, cols, cols)), (attn_2[0],)
-    )
-    attn_keep, attn_send, small_total = finish_sums(
-        yhi_index, attn_terms, cols, (expand_w_grad,)
-    )
-    block_out = output_layer(own_rows, branch, attn_send)
+    feed_keep, feed_send, small_total = finish_sums(
+        yhi_index, feed_terms, 2 * cols, (attn_2[0], block_out, input_grad)
+    )
+    attn_keep, attn_send = finish_sums(yhi_index, attn_terms, cols, (feed_send,))
+    attn_got = swap(attn_send, "yhi")
     small_total = unfold(small_total)
     norm_total = lax.dynamic_slice_in_dim(
         small_total[:4].reshape(2, width), at_plane * 8 * unit, 8 * unit, 1
     ).reshape(2, 2, 4 * unit)
     norm_keep, norm_send = pick(first_yhi, norm_total[:, 0], norm_total[:, 1])
-    rider = jnp.pad(norm_send.astype(BF), ((0, 14), (0, cols - 4 * unit)))
-    got = swap(jnp.concatenate([attn_send, rider], 0), "yhi")
+    rider = jnp.pad(norm_send.astype(BF), ((0, 14), (0, 2 * cols - 4 * unit)))
+    got = swap(jnp.concatenate([feed_send, rider], 0), "yhi")
     attn_w_grad, dense_w_grad = join_halves(
         yhi_index,
         attn_keep,
+        attn_got,
+        ((3, 0, heads), (1, 3 * heads, heads)),
+    )
+    expand_w_grad, reduce_w_grad = join_halves(
+        yhi_index,
+        feed_keep,
         got[:block_rows],
-        ((3, 0, heads), (1, 3 * heads, heads)),
-        (block_out,),
+        ((1, 0, cols), (1, cols, cols)),
+        (attn_w_grad,),
     )
     keep = norm_keep + got[block_rows : block_rows + 2, : 4 * unit].astype(F32)
     keep = keep.reshape(2, 2, 2, unit)

time: 304 us -> 303 us (level)
  waiting for transfers between devices: 83 us -> 70.7 us
  starting transfers between devices: 54.7 us -> 62.1 us
    ppermute x15 -> x18, starting transfers between devices: 13.4 us -> 22.5 us  [move(): return lax.ppermute(value, ('x', 'z', 'core'), ring_pairs(first_ring, step))]
    ppermute x12, waiting for transfers between devices: 40 us -> 32 us  [swap(): return lax.ppermute(value, axis, [(0, 1), (1, 0)])]
    all_gather x1 -> x2, waiting for transfers between devices: 20.2 us -> 15.5 us  [the longest x1 15.5 us: body(): lax.all_gather(block[:, 2 * cols:], ('x', 'z'), axis=0, tiled=True)]
    reduce_scatter x1, waiting for transfers between devices: 0.01 us -> 3.09 us  [body(): lax.psum_scatter(normed_part, COLUMN, scatter_dimension=0, tiled=True)]
    ppermute x15 -> x18, waiting for transfers between devices: 20.2 us -> 18.1 us  [move(): return lax.ppermute(value, ('x', 'z', 'core'), ring_pairs(first_ring, step))]
    unnamed x129 -> x114, local copies, waits for them, and re-layouts: 17.6 us -> 18.2 us
  transfers between devices with their start and end apart: 38 -> 42, of which waited for: 16 -> 12; matrix products, arithmetic and copies ran while one was open for 5% -> 5% of each run, Pallas kernels for 24% -> 38%
where the time goes in v1:
time: 303 us; the launch traced here: 302 us
  Pallas kernels  120 us (40%)
  waiting for transfers between devices  70.7 us (23%)
  starting transfers between devices  62.1 us (20%)
  local copies, waits for them, and re-layouts  25.7 us (8%)
  between operations  14.6 us (5%)
  other arithmetic  8.58 us (3%)
    pallas_call x19, Pallas kernels, kernel_call(): return pl.pallas_call(run, **options)(*operands, *waits)  118 us
    ppermute x12, waiting for transfers between devices, swap(): return lax.ppermute(value, axis, [(0, 1), (1, 0)])  32 us
    ppermute x12, starting transfers between devices, swap(): return lax.ppermute(value, axis, [(0, 1), (1, 0)])  25.4 us
    ppermute x18, starting transfers between devices, move(): return lax.ppermute(value, ('x', 'z', 'core'), ring_pairs(first_ring, step))  22.5 us
    unnamed x114, local copies, waits for them, and re-layouts  18.2 us
    ppermute x18, waiting for transfers between devices, move(): return lax.ppermute(value, ('x', 'z', 'core'), ring_pairs(first_ring, step))  18.1 us
    all_gather x1, waiting for transfers between devices, body(): lax.all_gather(block[:, 2 * cols:], ('x', 'z'), axis=0, tiled=True)  15.5 us
    ppermute x4, starting transfers between devices, body(): small = small + lax.ppermute(small, axis, axis_swaps(odd))  8.56 us
  transfers between devices with their start and end apart: 42, of which 12 were waited for; matrix products, arithmetic and copies ran while one was open for 5% of the time, Pallas kernels for 38%

profile of v1, /device:TPU:1, one launch (start us, length us, event | category | flops | bytes accessed | tf_op | source)
XLA Modules:
  0.0 301.9 jit_solution(9735995998927992009)
XLA Ops:
  7.3 2.2 split_columns.1
  9.5 3.7 %collective-permute-start = (bf16[64,3072]{1,0:T(8,128)(2,1)}, bf16[64,3072]{1,0:T(8,128)(2,1)S(1)}, u32[]{:S(2)}, u32[]{:S(2)}) collective-permute-start(bf16[64,3072]{1,0:T(8,128)(2,1)} %get-tuple-element.67), channel_id=1, source_target_pairs={{0,64},{64,0},{1,65},{65,1},{2,66},{66,2},{3,67},{67,3},{4,68},{68... | collective-permute-start | bytes 1179656 | tf_op jit(solution)/shard_map/ppermute | solution.py:47
  13.3 8.8 %collective-permute-done.refs_2_ = bf16[64,3072]{1,0:T(8,128)(2,1)S(1)} collective-permute-done((bf16[64,3072]{1,0:T(8,128)(2,1)}, bf16[64,3072]{1,0:T(8,128)(2,1)S(1)}, u32[]{:S(2)}, u32[]{:S(2)}) %collective-permute-start) | collective-permute-done | bytes 393248 | tf_op jit(solution)/shard_map/ppermute | solution.py:47
  25.5 1.4 collective-permute-start.9
  26.9 1.5 collective-permute-start.11
  29.3 1.8 collective-permute-start.1
  32.9 18.8 %collective-permute-done.1 = bf16[16,1024]{1,0:T(8,128)(2,1)S(1)} collective-permute-done((bf16[16,1024]{1,0:T(8,128)(2,1)S(1)}, bf16[16,1024]{1,0:T(8,128)(2,1)S(1)}, u32[]{:S(2)}, u32[]{:S(2)}) %collective-permute-start.1) | collective-permute-done | bytes 32800 | tf_op jit(solution)/shard_map/ppermute | solution.py:47
  55.2 2.0 collective-permute-start.3
  57.1 1.7 collective-permute-start.14
  59.2 1.4 collective-permute-start.4
  60.8 1.7 collective-permute-done.4
  62.5 3.9 %collective-permute-start.5 = (bf16[16,1024]{1,0:T(8,128)(2,1)S(1)}, bf16[16,1024]{1,0:T(8,128)(2,1)S(1)}, u32[]{:S(2)}, u32[]{:S(2)}) collective-permute-start(bf16[16,1024]{1,0:T(8,128)(2,1)S(1)} %add.185), channel_id=1, source_target_pairs={{0,12},{4,8},{8,4},{12,0},{1,13},{5,9},{9,5},{13,1},{2,14},{6,10},... | collective-permute-start | bytes 98312 | tf_op jit(solution)/shard_map/ppermute | solution.py:1018
  66.4 6.5 %collective-permute-start.8 = (bf16[2,128,2048]{2,1,0:T(8,128)(2,1)S(1)}, bf16[2,128,2048]{2,1,0:T(8,128)(2,1)S(1)}, u32[]{:S(2)}, u32[]{:S(2)}) collective-permute-start(bf16[2,128,2048]{2,1,0:T(8,128)(2,1)S(1)} %pair_columns.1.refs_3_.refs_0_.refs_1_), channel_id=1, source_target_pairs={{0,1},{1,0},{2,3},{3,2},{4,5},{5,4},{6,7},{7,6},{8,9},{9,8},{10,11... | collective-permute-start | bytes 3145736 | tf_op jit(solution)/shard_map/ppermute | solution.py:47
  76.3 2.8 collective-permute-done.6
  79.1 1.4 collective-permute-start.7
  80.6 3.2 %fusion = (f32[1024,128]{1,0:T(8,128)}, f32[1024,128]{1,0:T(8,128)}, f32[1024,128]{1,0:T(8,128)}) fusion(f32[128]{0:T(128)S(1)} %copy-done.40, f32[1024]{0:T(1024)S(1)} %subtract_convert_fusion, pred[128]{0:T(512)(128)(4,1)S(1)} %copy-done.41, pred[128]{0:T(512)(128)(4,1)S(1)} %copy-done.42, pred[128]{0:T(512)(128)(4,1)S(1)} %copy-done.43), kind=kLoop, calls=%fused_computation.4 | loop fusion | flops 655360 | bytes 1577856 | tf_op jit(solution)/shard_map/jit(_where)/select_n | solution.py:1048
  87.5 12.1 %rows.1 = (bf16[1024,2048]{1,0:T(8,128)(2,1)}, bf16[1024,2048]{1,0:T(8,128)(2,1)}, bf16[1024,2048]{1,0:T(8,128)(2,1)}, bf16[1024,2048]{1,0:T(8,128)(2,1)}, bf16[...) custom-call(s32[5]{0:T(128)} %stack.62.refs_0_, s32[16]{0:T(128)} %fusion.17.refs_1_, ...), custom_call_target="tpu_custom_call" | custom-call | bytes 29360128 | tf_op jit(solution)/shard_map/rows/pallas_call | solution.py:92
  99.6 17.2 %expand.1 = (bf16[1024,1024]{1,0:T(8,128)(2,1)}, bf16[1024,1024]{1,0:T(8,128)(2,1)}, f32[1024,768]{1,0:T(8,128)}, bf16[1024,256]{1,0:T(8,128)(2,1)}) custom-call(bf16[2048,2048]{1,0:T(8,128)(2,1)} %all-gather.3.cloned.1.call-done.refs_0_.refs_1_.refs_2_, bf16[2048,2048]{1,0:T(8,128)(2,1)} %all-gather.3.cloned.1.call-done.refs_0_.refs_1_.refs_2_, ...), custom_call_target="tpu_custom_call" | custom-call | flops 7516192768 | bytes 8388608 | tf_op jit(solution)/shard_map/expand/pallas_call | solution.py:92
  116.8 11.9 %attention.1 = (bf16[1024,256]{1,0:T(8,128)(2,1)}, bf16[1024,768]{1,0:T(8,128)(2,1)}, f32[2,1,768]{2,1,0:T(1,128)}) custom-call(f32[1024,768]{1,0:T(8,128)} %get-tuple-element.75.refs_0_, bf16[1024,256]{1,0:T(8,128)(2,1)} %get-tuple-element.76.refs_1_, f32[1024,128]{1,0:T(8,128)} %get-tuple-element.130.refs_11_.refs_2_, ...), custom_call_target="tpu_custom_call" | custom-call | flops 1879048192 | bytes 8388608 | tf_op jit(solution)/shard_map/attention/pallas_call | solution.py:92
  128.7 9.2 %weight_grad.1 = (bf16[512,1024]{1,0:T(8,128)(2,1)}, bf16[512,1024]{1,0:T(8,128)(2,1)}, bf16[512,1024]{1,0:T(8,128)(2,1)}, bf16[512,1024]{1,0:T(8,128)(2,1)}) custom-call(bf16[1024,2048]{1,0:T(8,128)(2,1)} %get-tuple-element.70.refs_0_.refs_3_, bf16[1024,2048]{1,0:T(8,128)(2,1)} %get-tuple-element.71.refs_1_.refs_5_, ...), custom_call_target="tpu_custom_call" | custom-call | flops 4294967296 | bytes 14680064 | tf_op jit(solution)/shard_map/weight_grad/pallas_call | solution.py:92
  137.9 2.7 collective-permute-start.16
  140.6 15.5 %all-gather.5.cloned.1.call-done.refs_2_.refs_0_ = bf16[2048,1024]{1,0:T(8,128)(2,1)} async-done(((bf16[128,1024]{1,0:T(8,128)(2,1)}), bf16[2048,1024]{1,0:T(8,128)(2,1)}) %all-gather.5.cloned.1.call-update) | async-done | bytes 4194320 | tf_op jit(solution)/shard_map/all_gather | solution.py:1001
  156.1 10.1 %branch.1.refs_2_ = bf16[1024,2048]{1,0:T(8,128)(2,1)} custom-call(s32[1]{0:T(128)} %bitcast.23.refs_0_, bf16[2048,2048]{1,0:T(8,128)(2,1)} %all-gather.3.cloned.1.call-done.refs_0_.refs_1_.refs_2_, bf16[2048,1024]{1,0:T(8,128)(2,1)} %all-gather.5.cloned.1.call-done.refs_2_.refs_0_, bf16[1024,1024]{1,0:T(8,128)(2,1)} %get-tuple-element.81.refs_3_.refs_4_, ...), custom_call_target="tpu_custom_call" | custom-call | flops 5368709120 | bytes 12058624 | tf_op jit(solution)/shard_map/branch/pallas_call | solution.py:92
  167.6 2.5 add_pairs.2
  170.1 2.4 collective-permute-start.20
  172.5 20.9 %feed_back.1 = (bf16[1024,1024]{1,0:T(8,128)(2,1)}, f32[1,1024]{1,0:T(1,128)}, bf16[512,1024]{1,0:T(8,128)(2,1)}, bf16[512,1024]{1,0:T(8,128)(2,1)}, bf16[512,10...) custom-call(bf16[2048,1024]{1,0:T(8,128)(2,1)} %all-gather.5.cloned., ...), custom_call_target="tpu_custom_call" | custom-call | flops 12884901888 | bytes 41943040 | tf_op jit(solution)/shard_map/feed_back/pallas_call | solution.py:92
  193.5 2.7 collective-permute-start.19
  196.2 1.4 collective-permute-start.22
  198.6 13.7 %normed_grad.1 = (bf16[1024,2048]{1,0:T(8,128)(2,1)}, f32[2,2048]{1,0:T(2,128)}) custom-call(bf16[2048,2048]{1,0:T(8,128)(2,1)} %all-gather.3.cloned.1.call-done.refs_0_.refs_1_.refs_2_, bf16[2048,2048]{1,0:T(8,128)(2,1)} %all-gather.3.cloned.1.call-done.refs_0_.refs_1_.refs_2_, bf16[1024,768]{1,0:T(8,128)(2,1)} %get-tuple-element.77.refs_2_, ...), custom_call_target="tpu_custom_call" | custom-call | flops 7516192768 | bytes 19398656 | tf_op jit(solution)/shard_map/normed_grad/pallas_call | solution.py:92
  212.3 7.2 %collective-permute-done.21.refs_5_.refs_1_ = bf16[4,128,1024]{2,1,0:T(8,128)(2,1)S(1)} collective-permute-done((bf16[4,128,1024]{2,1,0:T(8,128)(2,1)}, bf16[4,128,1024]{2,1,0:T(8,128)(2,1)S(1)}, u32[]{:S(2)}, u32[]{:S(2)}) %collective-permute-start.21) | collective-permute-done | bytes 1048608 | tf_op jit(solution)/shard_map/ppermute | solution.py:34
  221.1 3.3 %add_pairs.3 = (bf16[512,1024]{1,0:T(8,128)(2,1)}, bf16[512,1024]{1,0:T(8,128)(2,1)}, bf16[1024,2048]{1,0:T(8,128)(2,1)}) custom-call(bf16[512,1024]{1,0:T(8,128)(2,1)} %get-tuple-element.87.refs_0_, bf16[512,1024]{1,0:T(8,128)(2,1)} %bitcast.89, bf16[512,1024]{1,0:T(8,128)(2,1)} %get-tuple-element.89.refs_2_, ...), custom_call_target="tpu_custom_call", output_to_operand_aliasing={{2}: (4, {})} | custom-call | bytes 6291456 | tf_op jit(solution)/shard_map/add_pairs/pallas_call | solution.py:92
  225.6 3.0 collective-permute-start.24
  230.2 1.5 collective-permute-start.27
  232.4 9.6 %collective-permute-done.27 = f32[16,1024]{1,0:T(8,128)S(1)} collective-permute-done((f32[16,1024]{1,0:T(8,128)S(1)}, f32[16,1024]{1,0:T(8,128)S(1)}, u32[]{:S(2)}, u32[]{:S(2)}) %collective-permute-start.27) | collective-permute-done | bytes 65568 | tf_op jit(solution)/shard_map/ppermute | solution.py:34
  244.8 4.4 %add_lines.2 = (bf16[128,2176]{1,0:T(8,128)(2,1)}, bf16[128,2176]{1,0:T(8,128)(2,1)}, bf16[128,2176]{1,0:T(8,128)(2,1)}, bf16[128,2176]{1,0:T(8,128)(2,1)}) custom-call(bf16[4,128,1024]{2,1,0:T(8,128)(2,1)} %bitcast.93, bf16[4,128,1024]{2,1,0:T(8,128)(2,1)} %copy-done.19, bf16[4,128,1024]{2,1,0:T(8,128)(2,1)} %copy-done.26, bf16[4,128,1024]{2,1,0:T(8,128)(2,1)} %bitcast.94, ...), custom_call_target="tpu_custom_call" | custom-call | bytes 8912896 | tf_op jit(solution)/shard_map/add_lines/pallas_call | solution.py:92
  249.2 1.7 collective-permute-start.28
  250.9 2.3 collective-permute-start.30
  253.2 2.8 add_lines.3
  256.0 1.5 collective-permute-start.34
  260.8 3.1 %reduce-scatter.5.cloned.1.call-done.refs_2_ = bf16[128,2048]{1,0:T(8,128)(2,1)} async-done(((bf16[1024,2048]{1,0:T(8,128)(2,1)}), bf16[128,2048]{1,0:T(8,128)(2,1)}) %reduce-scatter.5.cloned.1.call-update) | async-done | bytes 524304 | tf_op jit(solution)/shard_map/reduce_scatter | solution.py:1094
  266.7 1.8 input_grad.1.refs_15_
  268.5 2.5 collective-permute-start.36
  273.8 2.1 collective-permute-start.31
  279.8 1.6 collective-permute-done.31
  281.4 4.3 %collective-permute-start.32 = (f32[2,2,16]{2,1,0:T(2,128)S(1)}, f32[2,2,16]{2,1,0:T(2,128)S(1)}, u32[]{:S(2)}, u32[]{:S(2)}) collective-permute-start(f32[2,2,16]{2,1,0:T(2,128)S(1)} %select_bitcast_fusion), channel_id=1, source_target_pairs={{0,2},{2,0},{1,3},{3,1},{4,6},{6,4},{5,7},{7,5},{8,10},{10,8},{9,1... | collective-permute-start | bytes 776 | tf_op jit(solution)/shard_map/ppermute | solution.py:47
  286.4 1.8 join_halves.2
  288.9 3.3 %collective-permute-start.33 = (f32[2,16]{1,0:T(2,128)S(1)}, f32[2,16]{1,0:T(2,128)S(1)}, u32[]{:S(2)}, u32[]{:S(2)}) collective-permute-start(f32[2,16]{1,0:T(2,128)S(1)} %bitcast.117), channel_id=1, source_target_pairs={{0,1},{1,0},{2,3},{3,2},{4,5},{5,4},{6,7},{7,6},{8,9},{9,8},{10,11... | collective-permute-start | bytes 392 | tf_op jit(solution)/shard_map/ppermute | solution.py:47
  292.2 2.1 join_halves.3
  (245 shorter events, 42.6 us)
Async XLA Ops:
  7.2 92.4 %all-gather.3.cloned.1.call-start = ((), (), s32[]{:S(2)}) async-start(), calls=%async_computation.2 | async-start | bytes 8912896 | tf_op jit(solution)/shard_map/all_gather | solution.py:1000
  9.5 12.5 %collective-permute-start = (bf16[64,3072]{1,0:T(8,128)(2,1)}, bf16[64,3072]{1,0:T(8,128)(2,1)S(1)}, u32[]{:S(2)}, u32[]{:S(2)}) collective-permute-start(bf16[64,3072]{1,0:T(8,128)(2,1)} %get-tuple-element.67), channel_id=1, source_target_pairs={{0,64},{64,0},{1,65},{65,1},{2,66},{66,2},{3,67},{67,3},{4,68},{68... | collective-permute-start | bytes 1179656 | tf_op jit(solution)/shard_map/ppermute | solution.py:47
  24.0 51.8 %copy-start.38 = (pred[16]{0:T(512)(128)(4,1)S(1)}, pred[16]{0:T(512)(128)(4,1)}, u32[]{:S(2)}) copy-start(pred[16]{0:T(512)(128)(4,1)} %constant.185) | copy-start | bytes 52
  24.0 132.1 %all-gather.5.cloned.1.call-start = ((), (), s32[]{:S(2)}) async-start(), calls=%async_computation.3 | async-start | bytes 4456448 | tf_op jit(solution)/shard_map/all_gather | solution.py:1001
  24.8 55.8 %copy-start.40 = (f32[128]{0:T(128)S(1)}, f32[128]{0:T(128)}, u32[]{:S(2)}) copy-start(f32[128]{0:T(128)} %constant.187) | copy-start | bytes 1540
  24.8 55.8 %copy-start.41 = (pred[128]{0:T(512)(128)(4,1)S(1)}, pred[128]{0:T(512)(128)(4,1)}, u32[]{:S(2)}) copy-start(pred[128]{0:T(512)(128)(4,1)} %constant.189) | copy-start | bytes 388
  24.8 55.8 %copy-start.42 = (pred[128]{0:T(512)(128)(4,1)S(1)}, pred[128]{0:T(512)(128)(4,1)}, u32[]{:S(2)}) copy-start(pred[128]{0:T(512)(128)(4,1)} %constant.188) | copy-start | bytes 388
  24.8 55.8 %copy-start.43 = (pred[128]{0:T(512)(128)(4,1)S(1)}, pred[128]{0:T(512)(128)(4,1)}, u32[]{:S(2)}) copy-start(pred[128]{0:T(512)(128)(4,1)} %constant.186) | copy-start | bytes 388
  24.8 232.7 %reduce-scatter.3.cloned.1.call-start = ((), (), s32[]{:S(2)}) async-start(), calls=%async_computation.4 | async-start | bytes 4718592 | tf_op jit(solution)/shard_map/reduce_scatter | solution.py:1093
  25.5 61.9 %copy-start = (bf16[2,128,2048]{2,1,0:T(8,128)(2,1)}, bf16[2,128,2048]{2,1,0:T(8,128)(2,1)S(1)}, u32[]{:S(2)}) copy-start(bf16[2,128,2048]{2,1,0:T(8,128)(2,1)S(1)} %pair_columns.1.refs_3_.refs_0_.refs_1_) | copy-start | bytes 3145732
  25.5 27.5 %collective-permute-start.9 = (bf16[2,128,2048]{2,1,0:T(8,128)(2,1)S(1)}, bf16[2,128,2048]{2,1,0:T(8,128)(2,1)S(1)}, u32[]{:S(2)}, u32[]{:S(2)}) collective-permute-start(bf16[2,128,2048]{2,1,0:T(8,128)(2,1)S(1)} %pair_columns.1.refs_3_.refs_0_.refs_1_), channel_id=1, source_target_pairs={{0,2},{2,64},{64,66},{66,0},{1,3},{3,65},{65,67},{67,1},{4,6},{6,6... | collective-permute-start | bytes 3145736 | tf_op jit(solution)/shard_map/ppermute | solution.py:43
  26.9 26.2 %collective-permute-start.11 = (bf16[2,128,2048]{2,1,0:T(8,128)(2,1)S(1)}, bf16[2,128,2048]{2,1,0:T(8,128)(2,1)S(1)}, u32[]{:S(2)}, u32[]{:S(2)}) collective-permute-start(bf16[2,128,2048]{2,1,0:T(8,128)(2,1)S(1)} %pair_columns.1.refs_3_.refs_0_.refs_1_), channel_id=1, source_target_pairs={{0,66},{2,0},{64,2},{66,64},{1,67},{3,1},{65,3},{67,65},{4,70},{6,... | collective-permute-start | bytes 3145736 | tf_op jit(solution)/shard_map/ppermute | solution.py:43
  29.3 22.3 %collective-permute-start.1 = (bf16[16,1024]{1,0:T(8,128)(2,1)S(1)}, bf16[16,1024]{1,0:T(8,128)(2,1)S(1)}, u32[]{:S(2)}, u32[]{:S(2)}) collective-permute-start(bf16[16,1024]{1,0:T(8,128)(2,1)S(1)} %dynamic_update_slice.13), channel_id=1, source_target_pairs={{0,64},{64,0},{1,65},{65,1},{2,66},{66,2},{3,67},{67,3},{4,68},{68... | collective-permute-start | bytes 98312 | tf_op jit(solution)/shard_map/ppermute | solution.py:47
  51.7 3.5 %collective-permute-start.2 = (bf16[16,1024]{1,0:T(8,128)(2,1)S(1)}, bf16[16,1024]{1,0:T(8,128)(2,1)S(1)}, u32[]{:S(2)}, u32[]{:S(2)}) collective-permute-start(bf16[16,1024]{1,0:T(8,128)(2,1)S(1)} %pad_maximum_fusion.1), channel_id=1, source_target_pairs={{0,16},{16,0},{32,48},{48,32},{1,17},{17,1},{33,49},{49,33},{2,18}... | collective-permute-start | bytes 98312 | tf_op jit(solution)/shard_map/ppermute | solution.py:1018
  54.2 18.7 %collective-permute-start.13 = (bf16[1,128,2048]{2,1,0:T(8,128)(2,1)}, bf16[1,128,2048]{2,1,0:T(8,128)(2,1)}, u32[]{:S(2)}, u32[]{:S(2)}) collective-permute-start(bf16[1,128,2048]{2,1,0:T(8,128)(2,1)} %get-tuple-element.68), channel_id=1, source_target_pairs={{0,2},{2,64},{64,66},{66,0},{1,3},{3,65},{65,67},{67,1},{4,6},{6,6... | collective-permute-start | bytes 1572872 | tf_op jit(solution)/shard_map/ppermute | solution.py:43
  55.2 4.1 %collective-permute-start.3 = (bf16[16,1024]{1,0:T(8,128)(2,1)S(1)}, bf16[16,1024]{1,0:T(8,128)(2,1)S(1)}, u32[]{:S(2)}, u32[]{:S(2)}) collective-permute-start(bf16[16,1024]{1,0:T(8,128)(2,1)S(1)} %fusion.22), channel_id=1, source_target_pairs={{0,48},{16,32},{32,16},{48,0},{1,49},{17,33},{33,17},{49,1},{2,50}... | collective-permute-start | bytes 98312 | tf_op jit(solution)/shard_map/ppermute | solution.py:1018
  57.1 17.4 %collective-permute-start.14 = (bf16[1,128,2048]{2,1,0:T(8,128)(2,1)}, bf16[1,128,2048]{2,1,0:T(8,128)(2,1)}, u32[]{:S(2)}, u32[]{:S(2)}) collective-permute-start(bf16[1,128,2048]{2,1,0:T(8,128)(2,1)} %get-tuple-element.69), channel_id=1, source_target_pairs={{0,66},{2,0},{64,2},{66,64},{1,67},{3,1},{65,3},{67,65},{4,70},{6,... | collective-permute-start | bytes 1572872 | tf_op jit(solution)/shard_map/ppermute | solution.py:43
  59.2 3.2 %collective-permute-start.4 = (bf16[16,1024]{1,0:T(8,128)(2,1)S(1)}, bf16[16,1024]{1,0:T(8,128)(2,1)S(1)}, u32[]{:S(2)}, u32[]{:S(2)}) collective-permute-start(bf16[16,1024]{1,0:T(8,128)(2,1)S(1)} %add.184), channel_id=1, source_target_pairs={{0,4},{4,0},{8,12},{12,8},{1,5},{5,1},{9,13},{13,9},{2,6},{6,2},{1... | collective-permute-start | bytes 98312 | tf_op jit(solution)/shard_map/ppermute | solution.py:1018
  62.5 13.3 %collective-permute-start.5 = (bf16[16,1024]{1,0:T(8,128)(2,1)S(1)}, bf16[16,1024]{1,0:T(8,128)(2,1)S(1)}, u32[]{:S(2)}, u32[]{:S(2)}) collective-permute-start(bf16[16,1024]{1,0:T(8,128)(2,1)S(1)} %add.185), channel_id=1, source_target_pairs={{0,12},{4,8},{8,4},{12,0},{1,13},{5,9},{9,5},{13,1},{2,14},{6,10},... | collective-permute-start | bytes 98312 | tf_op jit(solution)/shard_map/ppermute | solution.py:1018
  66.4 18.0 %collective-permute-start.8 = (bf16[2,128,2048]{2,1,0:T(8,128)(2,1)S(1)}, bf16[2,128,2048]{2,1,0:T(8,128)(2,1)S(1)}, u32[]{:S(2)}, u32[]{:S(2)}) collective-permute-start(bf16[2,128,2048]{2,1,0:T(8,128)(2,1)S(1)} %pair_columns.1.refs_3_.refs_0_.refs_1_), channel_id=1, source_target_pairs={{0,1},{1,0},{2,3},{3,2},{4,5},{5,4},{6,7},{7,6},{8,9},{9,8},{10,11... | collective-permute-start | bytes 3145736 | tf_op jit(solution)/shard_map/ppermute | solution.py:47
  72.9 11.5 %collective-permute-start.10 = (bf16[2,128,2048]{2,1,0:T(8,128)(2,1)S(1)}, bf16[2,128,2048]{2,1,0:T(8,128)(2,1)S(1)}, u32[]{:S(2)}, u32[]{:S(2)}) collective-permute-start(bf16[2,128,2048]{2,1,0:T(8,128)(2,1)S(1)} %collective-permute-done.9.refs_0_.refs_5_), channel_id=1, source_target_pairs={{0,1},{1,0},{2,3},{3,2},{4,5},{5,4},{6,7},{7,6},{8,9},{9,8},{10,11... | collective-permute-start | bytes 3145736 | tf_op jit(solution)/shard_map/ppermute | solution.py:47
  72.9 11.5 %collective-permute-start.12 = (bf16[2,128,2048]{2,1,0:T(8,128)(2,1)S(1)}, bf16[2,128,2048]{2,1,0:T(8,128)(2,1)S(1)}, u32[]{:S(2)}, u32[]{:S(2)}) collective-permute-start(bf16[2,128,2048]{2,1,0:T(8,128)(2,1)S(1)} %collective-permute-done.11.refs_1_.refs_7_), channel_id=1, source_target_pairs={{0,1},{1,0},{2,3},{3,2},{4,5},{5,4},{6,7},{7,6},{8,9},{9,8},{10,11... | collective-permute-start | bytes 3145736 | tf_op jit(solution)/shard_map/ppermute | solution.py:47
  75.7 8.8 %collective-permute-start.15 = (bf16[2,128,2048]{2,1,0:T(8,128)(2,1)S(1)}, bf16[2,128,2048]{2,1,0:T(8,128)(2,1)S(1)}, u32[]{:S(2)}, u32[]{:S(2)}) collective-permute-start(bf16[2,128,2048]{2,1,0:T(8,128)(2,1)S(1)} %constant_dynamic-update-slice_fusion.refs_9_), channel_id=1, source_target_pairs={{0,1},{1,0},{2,3},{3,2},{4,5},{5,4},{6,7},{7,6},{8,9},{9,8},{10,11... | collective-permute-start | bytes 3145736 | tf_op jit(solution)/shard_map/ppermute | solution.py:47
  75.9 3.2 %collective-permute-start.6 = (bf16[16,1024]{1,0:T(8,128)(2,1)S(1)}, bf16[16,1024]{1,0:T(8,128)(2,1)S(1)}, u32[]{:S(2)}, u32[]{:S(2)}) collective-permute-start(bf16[16,1024]{1,0:T(8,128)(2,1)S(1)} %get-tuple-element.122), channel_id=1, source_target_pairs={{0,2},{2,0},{1,3},{3,1},{4,6},{6,4},{5,7},{7,5},{8,10},{10,8},{9,1... | collective-permute-start | bytes 98312 | tf_op jit(solution)/shard_map/ppermute | solution.py:47
  79.1 4.6 %collective-permute-start.7 = (bf16[16,1024]{1,0:T(8,128)(2,1)S(1)}, bf16[16,1024]{1,0:T(8,128)(2,1)S(1)}, u32[]{:S(2)}, u32[]{:S(2)}) collective-permute-start(bf16[16,1024]{1,0:T(8,128)(2,1)S(1)} %fusion.21), channel_id=1, source_target_pairs={{0,1},{1,0},{2,3},{3,2},{4,5},{5,4},{6,7},{7,6},{8,9},{9,8},{10,11... | collective-permute-start | bytes 98312 | tf_op jit(solution)/shard_map/ppermute | solution.py:47
  137.9 28.3 %collective-permute-start.16 = (bf16[4,128,1024]{2,1,0:T(8,128)(2,1)}, bf16[4,128,1024]{2,1,0:T(8,128)(2,1)S(1)}, u32[]{:S(2)}, u32[]{:S(2)}) collective-permute-start(bf16[4,128,1024]{2,1,0:T(8,128)(2,1)} %bitcast.126), channel_id=1, source_target_pairs={{0,12},{1,49},{4,0},{5,53},{8,4},{9,57},{12,8},{13,61},{16,28},{17... | collective-permute-start | bytes 3145736 | tf_op jit(solution)/shard_map/ppermute | solution.py:34
  140.6 25.6 %collective-permute-start.17 = (bf16[4,128,1024]{2,1,0:T(8,128)(2,1)}, bf16[4,128,1024]{2,1,0:T(8,128)(2,1)S(1)}, u32[]{:S(2)}, u32[]{:S(2)}) collective-permute-start(bf16[4,128,1024]{2,1,0:T(8,128)(2,1)} %bitcast.125), channel_id=1, source_target_pairs={{0,4},{1,17},{4,8},{5,21},{8,12},{9,25},{12,0},{13,29},{16,20},{17... | collective-permute-start | bytes 3145736 | tf_op jit(solution)/shard_map/ppermute | solution.py:34
  170.0 93.9 %reduce-scatter.5.cloned.1.call-start = ((), (), s32[]{:S(2)}) async-start(), calls=%async_computation.5 | async-start | bytes 4718592 | tf_op jit(solution)/shard_map/reduce_scatter | solution.py:1094
  170.1 27.5 %collective-permute-start.20 = (bf16[4,128,1024]{2,1,0:T(8,128)(2,1)}, bf16[4,128,1024]{2,1,0:T(8,128)(2,1)S(1)}, u32[]{:S(2)}, u32[]{:S(2)}) collective-permute-start(bf16[4,128,1024]{2,1,0:T(8,128)(2,1)} %bitcast.26.refs_6_), channel_id=1, source_target_pairs={{0,12},{1,49},{4,0},{5,53},{8,4},{9,57},{12,8},{13,61},{16,28},{17... | collective-permute-start | bytes 3145736 | tf_op jit(solution)/shard_map/ppermute | solution.py:34
  193.4 18.9 %collective-permute-start.18 = (bf16[4,128,1024]{2,1,0:T(8,128)(2,1)}, bf16[4,128,1024]{2,1,0:T(8,128)(2,1)S(1)}, u32[]{:S(2)}, u32[]{:S(2)}) collective-permute-start(bf16[4,128,1024]{2,1,0:T(8,128)(2,1)} %bitcast.124), channel_id=1, source_target_pairs={{0,4},{1,17},{4,8},{5,21},{8,12},{9,25},{12,0},{13,29},{16,20},{17... | collective-permute-start | bytes 3145736 | tf_op jit(solution)/shard_map/ppermute | solution.py:34
  193.5 18.8 %collective-permute-start.19 = (bf16[4,128,1024]{2,1,0:T(8,128)(2,1)}, bf16[4,128,1024]{2,1,0:T(8,128)(2,1)S(1)}, u32[]{:S(2)}, u32[]{:S(2)}) collective-permute-start(bf16[4,128,1024]{2,1,0:T(8,128)(2,1)} %bitcast.123), channel_id=1, source_target_pairs={{0,12},{1,49},{4,0},{5,53},{8,4},{9,57},{12,8},{13,61},{16,28},{17... | collective-permute-start | bytes 3145736 | tf_op jit(solution)/shard_map/ppermute | solution.py:34
  196.1 23.3 %collective-permute-start.21 = (bf16[4,128,1024]{2,1,0:T(8,128)(2,1)}, bf16[4,128,1024]{2,1,0:T(8,128)(2,1)S(1)}, u32[]{:S(2)}, u32[]{:S(2)}) collective-permute-start(bf16[4,128,1024]{2,1,0:T(8,128)(2,1)} %bitcast.122), channel_id=1, source_target_pairs={{0,12},{1,49},{4,0},{5,53},{8,4},{9,57},{12,8},{13,61},{16,28},{17... | collective-permute-start | bytes 3145736 | tf_op jit(solution)/shard_map/ppermute | solution.py:34
  196.2 23.9 %collective-permute-start.22 = (bf16[4,128,1024]{2,1,0:T(8,128)(2,1)}, bf16[4,128,1024]{2,1,0:T(8,128)(2,1)S(1)}, u32[]{:S(2)}, u32[]{:S(2)}) collective-permute-start(bf16[4,128,1024]{2,1,0:T(8,128)(2,1)} %bitcast.121), channel_id=1, source_target_pairs={{0,4},{1,17},{4,8},{5,21},{8,12},{9,25},{12,0},{13,29},{16,20},{17... | collective-permute-start | bytes 3145736 | tf_op jit(solution)/shard_map/ppermute | solution.py:34
  225.6 17.8 %collective-permute-start.23 = (bf16[4,128,1024]{2,1,0:T(8,128)(2,1)S(1)}, bf16[4,128,1024]{2,1,0:T(8,128)(2,1)S(1)}, u32[]{:S(2)}, u32[]{:S(2)}) collective-permute-start(bf16[4,128,1024]{2,1,0:T(8,128)(2,1)S(1)} %bitcast.84), channel_id=1, source_target_pairs={{0,4},{1,17},{4,8},{5,21},{8,12},{9,25},{12,0},{13,29},{16,20},{17... | collective-permute-start | bytes 3145736 | tf_op jit(solution)/shard_map/ppermute | solution.py:34
  225.6 17.8 %collective-permute-start.24 = (bf16[4,128,1024]{2,1,0:T(8,128)(2,1)}, bf16[4,128,1024]{2,1,0:T(8,128)(2,1)S(1)}, u32[]{:S(2)}, u32[]{:S(2)}) collective-permute-start(bf16[4,128,1024]{2,1,0:T(8,128)(2,1)} %bitcast.120), channel_id=1, source_target_pairs={{0,12},{1,49},{4,0},{5,53},{8,4},{9,57},{12,8},{13,61},{16,28},{17... | collective-permute-start | bytes 3145736 | tf_op jit(solution)/shard_map/ppermute | solution.py:34
  230.2 11.7 %collective-permute-start.27 = (f32[16,1024]{1,0:T(8,128)S(1)}, f32[16,1024]{1,0:T(8,128)S(1)}, u32[]{:S(2)}, u32[]{:S(2)}) collective-permute-start(f32[16,1024]{1,0:T(8,128)S(1)} %maximum_maximum_fusion), channel_id=1, source_target_pairs={{0,12},{1,49},{4,0},{5,53},{8,4},{9,57},{12,8},{13,61},{16,28},{17... | collective-permute-start | bytes 196616 | tf_op jit(solution)/shard_map/ppermute | solution.py:34
  231.7 11.0 %collective-permute-start.26 = (f32[16,1024]{1,0:T(8,128)S(1)}, f32[16,1024]{1,0:T(8,128)S(1)}, u32[]{:S(2)}, u32[]{:S(2)}) collective-permute-start(f32[16,1024]{1,0:T(8,128)S(1)} %maximum_maximum_fusion), channel_id=1, source_target_pairs={{0,8},{1,33},{4,12},{5,37},{8,0},{9,41},{12,4},{13,45},{16,24},{17... | collective-permute-start | bytes 196616 | tf_op jit(solution)/shard_map/ppermute | solution.py:34
  231.7 11.0 %collective-permute-start.25 = (f32[16,1024]{1,0:T(8,128)S(1)}, f32[16,1024]{1,0:T(8,128)S(1)}, u32[]{:S(2)}, u32[]{:S(2)}) collective-permute-start(f32[16,1024]{1,0:T(8,128)S(1)} %maximum_maximum_fusion), channel_id=1, source_target_pairs={{0,4},{1,17},{4,8},{5,21},{8,12},{9,25},{12,0},{13,29},{16,20},{17... | collective-permute-start | bytes 196616 | tf_op jit(solution)/shard_map/ppermute | solution.py:34
  249.2 19.4 %collective-permute-start.28 = (bf16[128,2176]{1,0:T(8,128)(2,1)}, bf16[128,2176]{1,0:T(8,128)(2,1)S(1)}, u32[]{:S(2)}, u32[]{:S(2)}) collective-permute-start(bf16[128,2176]{1,0:T(8,128)(2,1)} %get-tuple-element.107), channel_id=1, source_target_pairs={{0,48},{1,13},{4,52},{5,1},{8,56},{9,5},{12,60},{13,9},{16,0},{17,... | collective-permute-start | bytes 1671176 | tf_op jit(solution)/shard_map/ppermute | solution.py:34
  250.9 20.2 %collective-permute-start.29 = (bf16[128,2176]{1,0:T(8,128)(2,1)}, bf16[128,2176]{1,0:T(8,128)(2,1)S(1)}, u32[]{:S(2)}, u32[]{:S(2)}) collective-permute-start(bf16[128,2176]{1,0:T(8,128)(2,1)} %get-tuple-element.108), channel_id=1, source_target_pairs={{0,16},{1,5},{4,20},{5,9},{8,24},{9,13},{12,28},{13,1},{16,32},{17... | collective-permute-start | bytes 1671176 | tf_op jit(solution)/shard_map/ppermute | solution.py:34
  250.9 20.2 %collective-permute-start.30 = (bf16[128,2176]{1,0:T(8,128)(2,1)}, bf16[128,2176]{1,0:T(8,128)(2,1)S(1)}, u32[]{:S(2)}, u32[]{:S(2)}) collective-permute-start(bf16[128,2176]{1,0:T(8,128)(2,1)} %get-tuple-element.109), channel_id=1, source_target_pairs={{0,32},{1,9},{4,36},{5,13},{8,40},{9,1},{12,44},{13,5},{16,48},{17... | collective-permute-start | bytes 1671176 | tf_op jit(solution)/shard_map/ppermute | solution.py:34
  256.0 20.0 %collective-permute-start.34 = (bf16[128,1024]{1,0:T(8,128)(2,1)}, bf16[128,1024]{1,0:T(8,128)(2,1)}, u32[]{:S(2)}, u32[]{:S(2)}) collective-permute-start(bf16[128,1024]{1,0:T(8,128)(2,1)} %get-tuple-element.112), channel_id=1, source_target_pairs={{0,48},{1,13},{4,52},{5,1},{8,56},{9,5},{12,60},{13,9},{16,0},{17,... | collective-permute-start | bytes 786440 | tf_op jit(solution)/shard_map/ppermute | solution.py:34
  257.4 18.6 %collective-permute-start.35 = (bf16[128,1024]{1,0:T(8,128)(2,1)}, bf16[128,1024]{1,0:T(8,128)(2,1)}, u32[]{:S(2)}, u32[]{:S(2)}) collective-permute-start(bf16[128,1024]{1,0:T(8,128)(2,1)} %get-tuple-element.113), channel_id=1, source_target_pairs={{0,16},{1,5},{4,20},{5,9},{8,24},{9,13},{12,28},{13,1},{16,32},{17... | collective-permute-start | bytes 786440 | tf_op jit(solution)/shard_map/ppermute | solution.py:34
  268.5 7.5 %collective-permute-start.36 = (bf16[128,1024]{1,0:T(8,128)(2,1)}, bf16[128,1024]{1,0:T(8,128)(2,1)S(1)}, u32[]{:S(2)}, u32[]{:S(2)}) collective-permute-start(bf16[128,1024]{1,0:T(8,128)(2,1)} %get-tuple-element.114), channel_id=1, source_target_pairs={{0,32},{1,9},{4,36},{5,13},{8,40},{9,1},{12,44},{13,5},{16,48},{17... | collective-permute-start | bytes 786440 | tf_op jit(solution)/shard_map/ppermute | solution.py:34
  273.8 7.5 %collective-permute-start.31 = (bf16[80,2048]{1,0:T(8,128)(2,1)S(1)}, bf16[80,2048]{1,0:T(8,128)(2,1)S(1)}, u32[]{:S(2)}, u32[]{:S(2)}) collective-permute-start(bf16[80,2048]{1,0:T(8,128)(2,1)S(1)} %fusion.6), channel_id=1, source_target_pairs={{0,64},{64,0},{1,65},{65,1},{2,66},{66,2},{3,67},{67,3},{4,68},{68... | collective-permute-start | bytes 983048 | tf_op jit(solution)/shard_map/ppermute | solution.py:47
  277.9 7.8 %collective-permute-start.37 = (bf16[64,1024]{1,0:T(8,128)(2,1)S(1)}, bf16[64,1024]{1,0:T(8,128)(2,1)S(1)}, u32[]{:S(2)}, u32[]{:S(2)}) collective-permute-start(bf16[64,1024]{1,0:T(8,128)(2,1)S(1)} %get-tuple-element.116), channel_id=1, source_target_pairs={{0,64},{64,0},{1,65},{65,1},{2,66},{66,2},{3,67},{67,3},{4,68},{68... | collective-permute-start | bytes 393224 | tf_op jit(solution)/shard_map/ppermute | solution.py:47
  281.4 7.5 %collective-permute-start.32 = (f32[2,2,16]{2,1,0:T(2,128)S(1)}, f32[2,2,16]{2,1,0:T(2,128)S(1)}, u32[]{:S(2)}, u32[]{:S(2)}) collective-permute-start(f32[2,2,16]{2,1,0:T(2,128)S(1)} %select_bitcast_fusion), channel_id=1, source_target_pairs={{0,2},{2,0},{1,3},{3,1},{4,6},{6,4},{5,7},{7,5},{8,10},{10,8},{9,1... | collective-permute-start | bytes 776 | tf_op jit(solution)/shard_map/ppermute | solution.py:47
  288.9 5.4 %collective-permute-start.33 = (f32[2,16]{1,0:T(2,128)S(1)}, f32[2,16]{1,0:T(2,128)S(1)}, u32[]{:S(2)}, u32[]{:S(2)}) collective-permute-start(f32[2,16]{1,0:T(2,128)S(1)} %bitcast.117), channel_id=1, source_target_pairs={{0,1},{1,0},{2,3},{3,2},{4,5},{5,4},{6,7},{7,6},{8,9},{9,8},{10,11... | collective-permute-start | bytes 392 | tf_op jit(solution)/shard_map/ppermute | solution.py:47
  (47 other events, 468.6 us)
Sparse Core Ops, SparseCore 0:
  24.1 74.8 all-gather.2
  101.7 54.3 all-gather.4
  170.2 37.2 reduce-scatter.2
  224.6 39.2 reduce-scatter.4
